TPU v7x, 768 devices: a whole 4x8x12 slice. The times are simulated.
768 devices in a mesh: row: 192 (over z, y, core), col: 4 (over x).
Axes of the slice: x: 4, y: 8, z: 12, core: 2. Of those that a mesh axis runs over, the one named last changes fastest.
Arguments:
- charges: bfloat16 [768, 128, 256], P('row'), may hold values from -6 to 6
- cluster_basis: bfloat16 [768, 32, 256], P('row'), may hold values from -0.375 to 0.375
- cluster_sizes: int32 [768], P('row'), may hold values from 128 to 256, as said below
- near_blocks: bfloat16 [12288, 256, 256], P(('row', 'col')), may hold values from -0.09375 to 0.09375
- near_rows: int32 [12288], P(('row', 'col')), may hold values from 0 to 767, as said below
- near_cols: int32 [12288], P(('row', 'col')), may hold values from 0 to 767, as said below
- near_live: int32 [768], P(('row', 'col')), may hold values from 1 to 16, as said below
- couplings: bfloat16 [98304, 32, 32], P(('row', 'col')), may hold values from -0.25 to 0.25
- far_rows: int32 [98304], P(('row', 'col')), may hold values from 0 to 767, as said below
- far_cols: int32 [98304], P(('row', 'col')), may hold values from 0 to 767, as said below
- far_live: int32 [768], P(('row', 'col')), may hold values from 0 to 128, as said below
Outputs:
- first_image: bfloat16 [768, 128, 256], P('row')
- second_image: bfloat16 [768, 128, 256], P('row')
Inputs may be any that keep to these rules, and one draw needn't show every extreme that they name: `cluster_sizes`: in every block of 4 clusters of one row index, some cluster uses all 256 panels. `near_rows`: slot s belongs to device s // 16, devices counted with row slowest and col fastest; its row cluster lies among the 4 clusters of that device's row index. `near_cols`: for a slot in use whose row cluster i lies in the block that starts at cluster b, the column cluster is at least i and below b + 8. Slots not in use hold any cluster. `near_live`: the used slots are the device's first ones. In each row index, one device uses all 16. `far_rows`: slot s belongs to device s // 128, devices counted with row slowest and col fastest; its row cluster lies among the 4 clusters of that device's row index. `far_cols`: for a slot in use whose row cluster lies in the block that starts at cluster b, the column cluster is at least b + 4 and below b + 32. Slots not in use hold any cluster. `far_live`: the used slots are the device's first ones. Devices of the last row index use none; in every other row index one device uses all 128.
All inputs are finite; a program needn't handle non-finite values.
Results may differ from a plain program's by a relative error of at most 0.022.
Values may be sent and summed in bfloat16 or wider, within the bound.
A program may use at most 64 MiB of HBM per device.

v0:
```python
import jax
import jax.numpy as jnp
from jax import lax
from jax.sharding import PartitionSpec as P

FAR_SLABS = 8


def shifted(x, axis, by):
    length = lax.axis_size(axis)
    pairs = [(i, i + by) for i in range(length) if 0 <= i + by < length]
    return lax.ppermute(x, axis, pairs)


def hot_sum(form, hot_table, values):
    upper = values.astype(jnp.bfloat16)
    lower = (values - upper.astype(jnp.float32)).astype(jnp.bfloat16)
    hot_table = hot_table.astype(jnp.bfloat16)
    first = jnp.einsum(form, hot_table, upper, preferred_element_type=jnp.float32)
    second = jnp.einsum(form, hot_table, lower, preferred_element_type=jnp.float32)
    return first + second


def near_terms(near_blocks, local_rows, local_cols, near_count, window_field, slab_size):
    block_group = 4
    rhs_width = window_field.shape[1]
    panel_width = window_field.shape[2]
    own_range = jnp.arange(slab_size, dtype=jnp.int32)
    wide_range = jnp.arange(2 * slab_size, dtype=jnp.int32)

    def one_group(group_number, totals):
        forward_total, backward_total = totals
        first_slot = group_number * block_group
        blocks = lax.dynamic_slice_in_dim(near_blocks, first_slot, block_group, 0)
        row_ids = lax.dynamic_slice_in_dim(local_rows, first_slot, block_group, 0)
        col_ids = lax.dynamic_slice_in_dim(local_cols, first_slot, block_group, 0)
        in_use = first_slot + jnp.arange(block_group, dtype=jnp.int32) < near_count
        row_field = jnp.take(window_field, row_ids, axis=0)
        col_field = jnp.take(window_field, col_ids, axis=0)
        forward = jnp.einsum("gpq,gkq->gkp", blocks, col_field, preferred_element_type=jnp.float32)
        backward = jnp.einsum("gpq,gkp->gkq", blocks, row_field, preferred_element_type=jnp.float32)
        row_hot = (row_ids[:, None] == own_range[None, :]) & in_use[:, None]
        col_hot = (col_ids[:, None] == wide_range[None, :]) & in_use[:, None]
        forward_total = forward_total + hot_sum("gc,gkp->ckp", row_hot, forward)
        backward_total = backward_total + hot_sum("gc,gkp->ckp", col_hot, backward)
        return (forward_total, backward_total)

    start_totals = (
        jnp.zeros((slab_size, rhs_width, panel_width), jnp.float32),
        jnp.zeros((2 * slab_size, rhs_width, panel_width), jnp.float32),
    )
    group_count = (near_count + block_group - 1) // block_group
    return lax.fori_loop(0, group_count, one_group, start_totals)


def far_terms(couplings, local_rows, local_cols, far_used, own_coef, ahead_coef):
    slab_size = own_coef.shape[0]
    ahead_size = ahead_coef.shape[0]
    row_coef = jnp.take(own_coef, local_rows, axis=0)
    col_coef = jnp.take(ahead_coef, local_cols, axis=0)
    forward = jnp.einsum("frt,ftk->frk", couplings, col_coef, preferred_element_type=jnp.float32)
    backward = jnp.einsum("ftr,ftk->frk", couplings, row_coef, preferred_element_type=jnp.float32)
    row_hot = (local_rows[:, None] == jnp.arange(slab_size, dtype=jnp.int32)[None, :]) & far_used[
        :, None
    ]
    col_hot = (local_cols[:, None] == jnp.arange(ahead_size, dtype=jnp.int32)[None, :]) & far_used[
        :, None
    ]
    own_part = hot_sum("fc,frk->crk", row_hot, forward)
    ahead_part = hot_sum("fc,frk->crk", col_hot, backward)
    return (own_part, ahead_part)


def fetch_ahead(send_coef):
    arrivals = []
    for offset in range(1, FAR_SLABS):
        arrivals.append(shifted(send_coef, "row", -offset))
    return jnp.concatenate(arrivals, axis=0)


def return_ahead(far_own, far_ahead):
    slab_size = far_own.shape[0]
    running = far_own
    for offset in range(1, FAR_SLABS):
        outgoing = far_ahead[(offset - 1) * slab_size : offset * slab_size]
        running = running + shifted(outgoing.astype(jnp.bfloat16), "row", offset).astype(
            outgoing.dtype
        )
    return running


def apply_operator(
    field_now,
    cluster_basis,
    panel_mask,
    near_blocks,
    near_local_rows,
    near_local_cols,
    near_count,
    couplings,
    far_local_rows,
    far_local_cols,
    far_used,
):
    slab_size = field_now.shape[0]
    coefficients = jnp.einsum(
        "crp,ckp->crk", cluster_basis, field_now, preferred_element_type=jnp.float32
    ).astype(jnp.bfloat16)
    next_field = shifted(field_now, "row", -1)
    ahead_coef = fetch_ahead(coefficients)
    window_field = jnp.concatenate([field_now, next_field], axis=0)
    near_forward, near_backward = near_terms(
        near_blocks, near_local_rows, near_local_cols, near_count, window_field, slab_size
    )
    far_own, far_ahead = far_terms(
        couplings, far_local_rows, far_local_cols, far_used, coefficients, ahead_coef
    )
    own_near = near_forward + near_backward[:slab_size]
    ahead_near = near_backward[slab_size:]
    own_near = own_near + shifted(ahead_near.astype(jnp.bfloat16), "row", 1).astype(
        ahead_near.dtype
    )
    far_total = return_ahead(far_own, far_ahead)
    own_near, far_total = (
        lax.psum(own_near.astype(jnp.bfloat16), "col").astype(jnp.float32),
        lax.psum(far_total.astype(jnp.bfloat16), "col").astype(jnp.float32),
    )
    far_rounded = far_total.astype(jnp.bfloat16)
    new_image = own_near + jnp.einsum(
        "crp,crk->ckp", cluster_basis, far_rounded, preferred_element_type=jnp.float32
    )
    new_image = jnp.where(panel_mask, new_image, jnp.zeros_like(new_image)).astype(jnp.bfloat16)
    return new_image


def per_device(
    charges,
    cluster_basis,
    cluster_sizes,
    near_blocks,
    near_rows,
    near_cols,
    near_live,
    couplings,
    far_rows,
    far_cols,
    far_live,
):
    slab_size = charges.shape[0]
    panel_width = charges.shape[2]
    first_cluster = lax.axis_index("row") * slab_size
    panel_mask = (
        lax.broadcasted_iota(jnp.int32, (slab_size, 1, panel_width), 2)
        < cluster_sizes[:, None, None]
    )
    near_local_rows = jnp.clip(near_rows - first_cluster, 0, slab_size - 1)
    near_local_cols = jnp.clip(near_cols - first_cluster, 0, 2 * slab_size - 1)
    far_local_rows = jnp.clip(far_rows - first_cluster, 0, slab_size - 1)
    far_local_cols = jnp.clip(
        far_cols - first_cluster - slab_size, 0, (FAR_SLABS - 1) * slab_size - 1
    )
    far_used = jnp.arange(far_rows.shape[0], dtype=jnp.int32) < far_live[0]
    near_count = near_live[0]
    masked = jnp.where(panel_mask, charges, jnp.zeros_like(charges))
    first_image = apply_operator(
        masked,
        cluster_basis,
        panel_mask,
        near_blocks,
        near_local_rows,
        near_local_cols,
        near_count,
        couplings,
        far_local_rows,
        far_local_cols,
        far_used,
    )
    second_image = apply_operator(
        first_image,
        cluster_basis,
        panel_mask,
        near_blocks,
        near_local_rows,
        near_local_cols,
        near_count,
        couplings,
        far_local_rows,
        far_local_cols,
        far_used,
    )
    return (first_image, second_image)


def solution(mesh):
    placed = (
        P("row", None, None),
        P("row", None, None),
        P("row"),
        P(("row", "col"), None, None),
        P(("row", "col")),
        P(("row", "col")),
        P(("row", "col")),
        P(("row", "col"), None, None),
        P(("row", "col")),
        P(("row", "col")),
        P(("row", "col")),
    )
    return jax.shard_map(
        per_device,
        mesh=mesh,
        in_specs=placed,
        out_specs=(P("row", None, None), P("row", None, None)),
        check_vma=False,
    )
```

profile of v0, /device:TPU:1, one launch (start us, length us, event | category | flops | bytes accessed | tf_op | source)
XLA Modules:
  0.0 354.8 jit_solution(11342948353095133494)
XLA Ops:
  9.2 12.4 %collective-permute-start.2 = (bf16[4,32,128]{2,1,0:T(8,128)(2,1)S(1)}, bf16[4,32,128]{2,1,0:T(8,128)(2,1)S(1)}, u32[]{:S(2)}, u32[]{:S(2)}) collective-permute-start(bf16[4,32,128]{2,1,0:T(8,128)(2,1)S(1)} %fusion.74), channel_id=1, source_target_pairs={{4,0},{8,4},{12,8},{16,12},{20,16},{24,20},{28,24},{32,28},{36,32}... | collective-permute-start | bytes 98312 | tf_op jit(solution)/shard_map/ppermute | solution.py:12
  34.4 2.4 copy.25
  40.1 1.9 collective-permute-start
  42.1 5.2 %collective-permute-start.10 = (bf16[4,32,128]{2,0,1:T(4,128)(2,1)}, bf16[4,32,128]{2,0,1:T(4,128)(2,1)}, u32[]{:S(2)}, u32[]{:S(2)}) collective-permute-start(bf16[4,32,128]{2,0,1:T(4,128)(2,1)} %get-tuple-element.270), channel_id=1, source_target_pairs={{0,8},{4,12},{8,16},{12,20},{16,24},{20,28},{24,32},{28,36},{32,40... | collective-permute-start | bytes 98312 | tf_op jit(solution)/shard_map/ppermute | solution.py:12
  47.3 6.7 %collective-permute-start.11 = (bf16[4,32,128]{2,0,1:T(4,128)(2,1)}, bf16[4,32,128]{2,0,1:T(4,128)(2,1)}, u32[]{:S(2)}, u32[]{:S(2)}) collective-permute-start(bf16[4,32,128]{2,0,1:T(4,128)(2,1)} %get-tuple-element.269), channel_id=1, source_target_pairs={{0,12},{4,16},{8,20},{12,24},{16,28},{20,32},{24,36},{28,40},{32,4... | collective-permute-start | bytes 98312 | tf_op jit(solution)/shard_map/ppermute | solution.py:12
  54.1 6.4 %collective-permute-start.12 = (bf16[4,32,128]{2,0,1:T(4,128)(2,1)}, bf16[4,32,128]{2,0,1:T(4,128)(2,1)}, u32[]{:S(2)}, u32[]{:S(2)}) collective-permute-start(bf16[4,32,128]{2,0,1:T(4,128)(2,1)} %get-tuple-element.268), channel_id=1, source_target_pairs={{0,16},{4,20},{8,24},{12,28},{16,32},{20,36},{24,40},{28,44},{32,4... | collective-permute-start | bytes 98312 | tf_op jit(solution)/shard_map/ppermute | solution.py:12
  60.4 4.6 %collective-permute-start.13 = (bf16[4,32,128]{2,0,1:T(4,128)(2,1)}, bf16[4,32,128]{2,0,1:T(4,128)(2,1)}, u32[]{:S(2)}, u32[]{:S(2)}) collective-permute-start(bf16[4,32,128]{2,0,1:T(4,128)(2,1)} %get-tuple-element.267), channel_id=1, source_target_pairs={{0,20},{4,24},{8,28},{12,32},{16,36},{20,40},{24,44},{28,48},{32,5... | collective-permute-start | bytes 98312 | tf_op jit(solution)/shard_map/ppermute | solution.py:12
  68.5 32.3 %while.26 = (s32[]{:T(128)}, f32[4,128,256]{2,0,1:T(4,128)}, f32[8,128,256]{2,0,1:T(8,128)S(1)}, s32[]{:T(128)}, s32[16]{0:T(128)S(1)}, /*index=5*/s32[]{:T(128)...) while((s32[]{:T(128)}, f32[4,128,256]{2,0,1:T(4,128)}, ...), condition=%wide.region_1.3_spmd.clone, body=%wide.region_0.2_spmd.clone.sunk | while | flops 142608656 | bytes 11019739 | solution.py:53
  74.4 2.2 fusion.185
  82.5 2.2 fusion.185
  90.6 2.2 fusion.185
  98.7 2.2 fusion.185
  101.2 2.1 collective-permute-start.1
  107.9 12.6 %collective-permute-start.9 = (bf16[4,32,128]{2,0,1:T(4,128)(2,1)S(1)}, bf16[4,32,128]{2,0,1:T(4,128)(2,1)S(1)}, u32[]{:S(2)}, u32[]{:S(2)}) collective-permute-start(bf16[4,32,128]{2,0,1:T(4,128)(2,1)S(1)} %get-tuple-element.264), channel_id=1, source_target_pairs={{0,4},{4,8},{8,12},{12,16},{16,20},{20,24},{24,28},{28,32},{32,36}... | collective-permute-start | bytes 98312 | tf_op jit(solution)/shard_map/ppermute | solution.py:12
  124.4 11.0 %psum.29 = bf16[4,32,128]{2,0,1:T(4,128)(2,1)S(1)} all-reduce(bf16[4,32,128]{2,0,1:T(4,128)(2,1)S(1)} %add_convert_fusion.1), channel_id=1, replica_groups=mesh['row'=192,'col'=4] {'col'}, use_global_device_ids=true, to_apply=%region_3.7 | all-reduce | flops 16384 | bytes 65536 | tf_op jit(solution)/shard_map/psum | solution.py:126
  135.4 45.6 %all-reduce.3.cloned.1.call-done = bf16[4,128,256]{2,1,0:T(8,128)(2,1)} async-done(((bf16[4,128,256]{2,1,0:T(8,128)(2,1)}), bf16[4,128,256]{2,1,0:T(8,128)(2,1)}) %all-reduce.3.cloned.1.call-update) | async-done | bytes 262160 | tf_op jit(solution)/shard_map/psum | solution.py:125
  182.4 4.4 %collective-permute-start.18 = (bf16[4,32,128]{2,1,0:T(8,128)(2,1)S(1)}, bf16[4,32,128]{2,1,0:T(8,128)(2,1)}, u32[]{:S(2)}, u32[]{:S(2)}) collective-permute-start(bf16[4,32,128]{2,1,0:T(8,128)(2,1)S(1)} %fusion.75), channel_id=1, source_target_pairs={{4,0},{8,4},{12,8},{16,12},{20,16},{24,20},{28,24},{32,28},{36,32}... | collective-permute-start | bytes 98312 | tf_op jit(solution)/shard_map/ppermute | solution.py:12
  201.4 1.9 collective-permute-start.16
  204.1 3.6 %collective-permute-start.25 = (bf16[4,32,128]{2,0,1:T(4,128)(2,1)}, bf16[4,32,128]{2,0,1:T(4,128)(2,1)}, u32[]{:S(2)}, u32[]{:S(2)}) collective-permute-start(bf16[4,32,128]{2,0,1:T(4,128)(2,1)} %get-tuple-element.257), channel_id=1, source_target_pairs={{0,4},{4,8},{8,12},{12,16},{16,20},{20,24},{24,28},{28,32},{32,36}... | collective-permute-start | bytes 98312 | tf_op jit(solution)/shard_map/ppermute | solution.py:12
  208.6 5.5 %collective-permute-start.26 = (bf16[4,32,128]{2,0,1:T(4,128)(2,1)}, bf16[4,32,128]{2,0,1:T(4,128)(2,1)}, u32[]{:S(2)}, u32[]{:S(2)}) collective-permute-start(bf16[4,32,128]{2,0,1:T(4,128)(2,1)} %get-tuple-element.263), channel_id=1, source_target_pairs={{0,8},{4,12},{8,16},{12,20},{16,24},{20,28},{24,32},{28,36},{32,40... | collective-permute-start | bytes 98312 | tf_op jit(solution)/shard_map/ppermute | solution.py:12
  214.8 5.6 %collective-permute-start.27 = (bf16[4,32,128]{2,0,1:T(4,128)(2,1)}, bf16[4,32,128]{2,0,1:T(4,128)(2,1)}, u32[]{:S(2)}, u32[]{:S(2)}) collective-permute-start(bf16[4,32,128]{2,0,1:T(4,128)(2,1)} %get-tuple-element.262), channel_id=1, source_target_pairs={{0,12},{4,16},{8,20},{12,24},{16,28},{20,32},{24,36},{28,40},{32,4... | collective-permute-start | bytes 98312 | tf_op jit(solution)/shard_map/ppermute | solution.py:12
  220.5 6.0 %collective-permute-start.28 = (bf16[4,32,128]{2,0,1:T(4,128)(2,1)}, bf16[4,32,128]{2,0,1:T(4,128)(2,1)}, u32[]{:S(2)}, u32[]{:S(2)}) collective-permute-start(bf16[4,32,128]{2,0,1:T(4,128)(2,1)} %get-tuple-element.261), channel_id=1, source_target_pairs={{0,16},{4,20},{8,24},{12,28},{16,32},{20,36},{24,40},{28,44},{32,4... | collective-permute-start | bytes 98312 | tf_op jit(solution)/shard_map/ppermute | solution.py:12
  230.0 32.3 %while.27 = (s32[]{:T(128)}, f32[4,128,256]{2,0,1:T(4,128)}, f32[8,128,256]{2,0,1:T(8,128)S(1)}, s32[]{:T(128)}, s32[16]{0:T(128)S(1)}, /*index=5*/s32[]{:T(128)...) while((s32[]{:T(128)}, f32[4,128,256]{2,0,1:T(4,128)}, ...), condition=%wide.region_5.9_spmd.clone, body=%wide.region_4.8_spmd.clone.sunk | while | flops 142608656 | bytes 11019739 | solution.py:53
  235.9 2.2 fusion.197
  244.0 2.2 fusion.197
  252.1 2.2 fusion.197
  260.1 2.2 fusion.197
  262.7 2.1 collective-permute-start.17
  267.2 11.2 %collective-permute-start.30 = (bf16[4,32,128]{2,0,1:T(4,128)(2,1)S(1)}, bf16[4,32,128]{2,0,1:T(4,128)(2,1)S(1)}, u32[]{:S(2)}, u32[]{:S(2)}) collective-permute-start(bf16[4,32,128]{2,0,1:T(4,128)(2,1)S(1)} %copy-done.12), channel_id=1, source_target_pairs={{0,24},{4,28},{8,32},{12,36},{16,40},{20,44},{24,48},{28,52},{32,5... | collective-permute-start | bytes 98312 | tf_op jit(solution)/shard_map/ppermute | solution.py:12
  283.5 17.2 %psum.31 = bf16[4,32,128]{2,0,1:T(4,128)(2,1)S(1)} all-reduce(bf16[4,32,128]{2,0,1:T(4,128)(2,1)S(1)} %add_convert_fusion), channel_id=1, replica_groups=mesh['row'=192,'col'=4] {'col'}, use_global_device_ids=true, to_apply=%region_7.11 | all-reduce | flops 16384 | bytes 65536 | tf_op jit(solution)/shard_map/psum | solution.py:126
  300.7 45.4 %all-reduce.5.cloned.1.call-done = bf16[4,128,256]{2,1,0:T(8,128)(2,1)} async-done(((bf16[4,128,256]{2,1,0:T(8,128)(2,1)}), bf16[4,128,256]{2,1,0:T(8,128)(2,1)}) %all-reduce.5.cloned.1.call-update) | async-done | bytes 262160 | tf_op jit(solution)/shard_map/psum | solution.py:125
  346.1 1.9 select_convert_fusion
  (266 shorter events, 105.0 us)
Async XLA Ops:
  7.2 173.8 %all-reduce.3.cloned.1.call-start = ((), (), s32[]{:S(2)}) async-start(), calls=%async_computation | async-start | bytes 524288 | tf_op jit(solution)/shard_map/psum | solution.py:125
  9.2 28.3 %collective-permute-start.2 = (bf16[4,32,128]{2,1,0:T(8,128)(2,1)S(1)}, bf16[4,32,128]{2,1,0:T(8,128)(2,1)S(1)}, u32[]{:S(2)}, u32[]{:S(2)}) collective-permute-start(bf16[4,32,128]{2,1,0:T(8,128)(2,1)S(1)} %fusion.74), channel_id=1, source_target_pairs={{4,0},{8,4},{12,8},{16,12},{20,16},{24,20},{28,24},{32,28},{36,32}... | collective-permute-start | bytes 98312 | tf_op jit(solution)/shard_map/ppermute | solution.py:12
  21.6 17.2 %collective-permute-start.3 = (bf16[4,32,128]{2,1,0:T(8,128)(2,1)S(1)}, bf16[4,32,128]{2,1,0:T(8,128)(2,1)S(1)}, u32[]{:S(2)}, u32[]{:S(2)}) collective-permute-start(bf16[4,32,128]{2,1,0:T(8,128)(2,1)S(1)} %fusion.74), channel_id=1, source_target_pairs={{8,0},{12,4},{16,8},{20,12},{24,16},{28,20},{32,24},{36,28},{40,32... | collective-permute-start | bytes 98312 | tf_op jit(solution)/shard_map/ppermute | solution.py:12
  22.9 17.2 %collective-permute-start.4 = (bf16[4,32,128]{2,1,0:T(8,128)(2,1)S(1)}, bf16[4,32,128]{2,1,0:T(8,128)(2,1)S(1)}, u32[]{:S(2)}, u32[]{:S(2)}) collective-permute-start(bf16[4,32,128]{2,1,0:T(8,128)(2,1)S(1)} %fusion.74), channel_id=1, source_target_pairs={{12,0},{16,4},{20,8},{24,12},{28,16},{32,20},{36,24},{40,28},{44,3... | collective-permute-start | bytes 98312 | tf_op jit(solution)/shard_map/ppermute | solution.py:12
  24.2 17.8 %collective-permute-start.5 = (bf16[4,32,128]{2,1,0:T(8,128)(2,1)S(1)}, bf16[4,32,128]{2,1,0:T(8,128)(2,1)S(1)}, u32[]{:S(2)}, u32[]{:S(2)}) collective-permute-start(bf16[4,32,128]{2,1,0:T(8,128)(2,1)S(1)} %fusion.74), channel_id=1, source_target_pairs={{16,0},{20,4},{24,8},{28,12},{32,16},{36,20},{40,24},{44,28},{48,3... | collective-permute-start | bytes 98312 | tf_op jit(solution)/shard_map/ppermute | solution.py:12
  25.5 21.8 %collective-permute-start.6 = (bf16[4,32,128]{2,1,0:T(8,128)(2,1)S(1)}, bf16[4,32,128]{2,1,0:T(8,128)(2,1)S(1)}, u32[]{:S(2)}, u32[]{:S(2)}) collective-permute-start(bf16[4,32,128]{2,1,0:T(8,128)(2,1)S(1)} %fusion.74), channel_id=1, source_target_pairs={{20,0},{24,4},{28,8},{32,12},{36,16},{40,20},{44,24},{48,28},{52,3... | collective-permute-start | bytes 98312 | tf_op jit(solution)/shard_map/ppermute | solution.py:12
  37.5 16.6 %collective-permute-start.7 = (bf16[4,32,128]{2,1,0:T(8,128)(2,1)S(1)}, bf16[4,32,128]{2,1,0:T(8,128)(2,1)S(1)}, u32[]{:S(2)}, u32[]{:S(2)}) collective-permute-start(bf16[4,32,128]{2,1,0:T(8,128)(2,1)S(1)} %fusion.74), channel_id=1, source_target_pairs={{24,0},{28,4},{32,8},{36,12},{40,16},{44,20},{48,24},{52,28},{56,3... | collective-permute-start | bytes 98312 | tf_op jit(solution)/shard_map/ppermute | solution.py:12
  38.8 21.7 %collective-permute-start.8 = (bf16[4,32,128]{2,1,0:T(8,128)(2,1)S(1)}, bf16[4,32,128]{2,1,0:T(8,128)(2,1)S(1)}, u32[]{:S(2)}, u32[]{:S(2)}) collective-permute-start(bf16[4,32,128]{2,1,0:T(8,128)(2,1)S(1)} %fusion.74), channel_id=1, source_target_pairs={{28,0},{32,4},{36,8},{40,12},{44,16},{48,20},{52,24},{56,28},{60,3... | collective-permute-start | bytes 98312 | tf_op jit(solution)/shard_map/ppermute | solution.py:12
  40.1 26.6 %collective-permute-start = (bf16[4,128,256]{2,1,0:T(8,128)(2,1)S(1)}, bf16[4,128,256]{2,1,0:T(8,128)(2,1)S(1)}, u32[]{:S(2)}, u32[]{:S(2)}) collective-permute-start(bf16[4,128,256]{2,1,0:T(8,128)(2,1)S(1)} %broadcast_select_fusion), channel_id=1, source_target_pairs={{4,0},{8,4},{12,8},{16,12},{20,16},{24,20},{28,24},{32,28},{36,32}... | collective-permute-start | bytes 786440 | tf_op jit(solution)/shard_map/ppermute | solution.py:12
  42.1 63.3 %collective-permute-start.10 = (bf16[4,32,128]{2,0,1:T(4,128)(2,1)}, bf16[4,32,128]{2,0,1:T(4,128)(2,1)}, u32[]{:S(2)}, u32[]{:S(2)}) collective-permute-start(bf16[4,32,128]{2,0,1:T(4,128)(2,1)} %get-tuple-element.270), channel_id=1, source_target_pairs={{0,8},{4,12},{8,16},{12,20},{16,24},{20,28},{24,32},{28,36},{32,40... | collective-permute-start | bytes 98312 | tf_op jit(solution)/shard_map/ppermute | solution.py:12
  47.3 59.3 %collective-permute-start.11 = (bf16[4,32,128]{2,0,1:T(4,128)(2,1)}, bf16[4,32,128]{2,0,1:T(4,128)(2,1)}, u32[]{:S(2)}, u32[]{:S(2)}) collective-permute-start(bf16[4,32,128]{2,0,1:T(4,128)(2,1)} %get-tuple-element.269), channel_id=1, source_target_pairs={{0,12},{4,16},{8,20},{12,24},{16,28},{20,32},{24,36},{28,40},{32,4... | collective-permute-start | bytes 98312 | tf_op jit(solution)/shard_map/ppermute | solution.py:12
  54.1 68.5 %collective-permute-start.12 = (bf16[4,32,128]{2,0,1:T(4,128)(2,1)}, bf16[4,32,128]{2,0,1:T(4,128)(2,1)}, u32[]{:S(2)}, u32[]{:S(2)}) collective-permute-start(bf16[4,32,128]{2,0,1:T(4,128)(2,1)} %get-tuple-element.268), channel_id=1, source_target_pairs={{0,16},{4,20},{8,24},{12,28},{16,32},{20,36},{24,40},{28,44},{32,4... | collective-permute-start | bytes 98312 | tf_op jit(solution)/shard_map/ppermute | solution.py:12
  60.4 62.1 %collective-permute-start.13 = (bf16[4,32,128]{2,0,1:T(4,128)(2,1)}, bf16[4,32,128]{2,0,1:T(4,128)(2,1)}, u32[]{:S(2)}, u32[]{:S(2)}) collective-permute-start(bf16[4,32,128]{2,0,1:T(4,128)(2,1)} %get-tuple-element.267), channel_id=1, source_target_pairs={{0,20},{4,24},{8,28},{12,32},{16,36},{20,40},{24,44},{28,48},{32,5... | collective-permute-start | bytes 98312 | tf_op jit(solution)/shard_map/ppermute | solution.py:12
  105.3 17.2 %collective-permute-start.14 = (bf16[4,32,128]{2,0,1:T(4,128)(2,1)S(1)}, bf16[4,32,128]{2,0,1:T(4,128)(2,1)S(1)}, u32[]{:S(2)}, u32[]{:S(2)}) collective-permute-start(bf16[4,32,128]{2,0,1:T(4,128)(2,1)S(1)} %copy-done.11), channel_id=1, source_target_pairs={{0,24},{4,28},{8,32},{12,36},{16,40},{20,44},{24,48},{28,52},{32,5... | collective-permute-start | bytes 98312 | tf_op jit(solution)/shard_map/ppermute | solution.py:12
  106.6 15.9 %collective-permute-start.15 = (bf16[4,32,128]{2,0,1:T(4,128)(2,1)S(1)}, bf16[4,32,128]{2,0,1:T(4,128)(2,1)S(1)}, u32[]{:S(2)}, u32[]{:S(2)}) collective-permute-start(bf16[4,32,128]{2,0,1:T(4,128)(2,1)S(1)} %copy-done.10), channel_id=1, source_target_pairs={{0,28},{4,32},{8,36},{12,40},{16,44},{20,48},{24,52},{28,56},{32,6... | collective-permute-start | bytes 98312 | tf_op jit(solution)/shard_map/ppermute | solution.py:12
  107.9 14.6 %collective-permute-start.9 = (bf16[4,32,128]{2,0,1:T(4,128)(2,1)S(1)}, bf16[4,32,128]{2,0,1:T(4,128)(2,1)S(1)}, u32[]{:S(2)}, u32[]{:S(2)}) collective-permute-start(bf16[4,32,128]{2,0,1:T(4,128)(2,1)S(1)} %get-tuple-element.264), channel_id=1, source_target_pairs={{0,4},{4,8},{8,12},{12,16},{16,20},{20,24},{24,28},{28,32},{32,36}... | collective-permute-start | bytes 98312 | tf_op jit(solution)/shard_map/ppermute | solution.py:12
  122.5 223.6 %all-reduce.5.cloned.1.call-start = ((), (), s32[]{:S(2)}) async-start(), calls=%async_computation.1 | async-start | bytes 524288 | tf_op jit(solution)/shard_map/psum | solution.py:125
  182.4 14.9 %collective-permute-start.18 = (bf16[4,32,128]{2,1,0:T(8,128)(2,1)S(1)}, bf16[4,32,128]{2,1,0:T(8,128)(2,1)}, u32[]{:S(2)}, u32[]{:S(2)}) collective-permute-start(bf16[4,32,128]{2,1,0:T(8,128)(2,1)S(1)} %fusion.75), channel_id=1, source_target_pairs={{4,0},{8,4},{12,8},{16,12},{20,16},{24,20},{28,24},{32,28},{36,32}... | collective-permute-start | bytes 98312 | tf_op jit(solution)/shard_map/ppermute | solution.py:12
  186.8 12.6 %collective-permute-start.19 = (bf16[4,32,128]{2,1,0:T(8,128)(2,1)S(1)}, bf16[4,32,128]{2,1,0:T(8,128)(2,1)}, u32[]{:S(2)}, u32[]{:S(2)}) collective-permute-start(bf16[4,32,128]{2,1,0:T(8,128)(2,1)S(1)} %fusion.75), channel_id=1, source_target_pairs={{8,0},{12,4},{16,8},{20,12},{24,16},{28,20},{32,24},{36,28},{40,32... | collective-permute-start | bytes 98312 | tf_op jit(solution)/shard_map/ppermute | solution.py:12
  188.1 13.4 %collective-permute-start.20 = (bf16[4,32,128]{2,1,0:T(8,128)(2,1)S(1)}, bf16[4,32,128]{2,1,0:T(8,128)(2,1)}, u32[]{:S(2)}, u32[]{:S(2)}) collective-permute-start(bf16[4,32,128]{2,1,0:T(8,128)(2,1)S(1)} %fusion.75), channel_id=1, source_target_pairs={{12,0},{16,4},{20,8},{24,12},{28,16},{32,20},{36,24},{40,28},{44,3... | collective-permute-start | bytes 98312 | tf_op jit(solution)/shard_map/ppermute | solution.py:12
  189.4 14.8 %collective-permute-start.21 = (bf16[4,32,128]{2,1,0:T(8,128)(2,1)S(1)}, bf16[4,32,128]{2,1,0:T(8,128)(2,1)}, u32[]{:S(2)}, u32[]{:S(2)}) collective-permute-start(bf16[4,32,128]{2,1,0:T(8,128)(2,1)S(1)} %fusion.75), channel_id=1, source_target_pairs={{16,0},{20,4},{24,8},{28,12},{32,16},{36,20},{40,24},{44,28},{48,3... | collective-permute-start | bytes 98312 | tf_op jit(solution)/shard_map/ppermute | solution.py:12
  190.7 17.9 %collective-permute-start.22 = (bf16[4,32,128]{2,1,0:T(8,128)(2,1)S(1)}, bf16[4,32,128]{2,1,0:T(8,128)(2,1)}, u32[]{:S(2)}, u32[]{:S(2)}) collective-permute-start(bf16[4,32,128]{2,1,0:T(8,128)(2,1)S(1)} %fusion.75), channel_id=1, source_target_pairs={{20,0},{24,4},{28,8},{32,12},{36,16},{40,20},{44,24},{48,28},{52,3... | collective-permute-start | bytes 98312 | tf_op jit(solution)/shard_map/ppermute | solution.py:12
  197.3 17.5 %collective-permute-start.23 = (bf16[4,32,128]{2,1,0:T(8,128)(2,1)S(1)}, bf16[4,32,128]{2,1,0:T(8,128)(2,1)S(1)}, u32[]{:S(2)}, u32[]{:S(2)}) collective-permute-start(bf16[4,32,128]{2,1,0:T(8,128)(2,1)S(1)} %fusion.75), channel_id=1, source_target_pairs={{24,0},{28,4},{32,8},{36,12},{40,16},{44,20},{48,24},{52,28},{56,3... | collective-permute-start | bytes 98312 | tf_op jit(solution)/shard_map/ppermute | solution.py:12
  199.4 21.1 %collective-permute-start.24 = (bf16[4,32,128]{2,1,0:T(8,128)(2,1)S(1)}, bf16[4,32,128]{2,1,0:T(8,128)(2,1)S(1)}, u32[]{:S(2)}, u32[]{:S(2)}) collective-permute-start(bf16[4,32,128]{2,1,0:T(8,128)(2,1)S(1)} %fusion.75), channel_id=1, source_target_pairs={{28,0},{32,4},{36,8},{40,12},{44,16},{48,20},{52,24},{56,28},{60,3... | collective-permute-start | bytes 98312 | tf_op jit(solution)/shard_map/ppermute | solution.py:12
  201.4 26.8 %collective-permute-start.16 = (bf16[4,128,256]{2,1,0:T(8,128)(2,1)S(1)}, bf16[4,128,256]{2,1,0:T(8,128)(2,1)S(1)}, u32[]{:S(2)}, u32[]{:S(2)}) collective-permute-start(bf16[4,128,256]{2,1,0:T(8,128)(2,1)S(1)} %select_convert_fusion.1), channel_id=1, source_target_pairs={{4,0},{8,4},{12,8},{16,12},{20,16},{24,20},{28,24},{32,28},{36,32}... | collective-permute-start | bytes 786440 | tf_op jit(solution)/shard_map/ppermute | solution.py:12
  204.1 61.7 %collective-permute-start.25 = (bf16[4,32,128]{2,0,1:T(4,128)(2,1)}, bf16[4,32,128]{2,0,1:T(4,128)(2,1)}, u32[]{:S(2)}, u32[]{:S(2)}) collective-permute-start(bf16[4,32,128]{2,0,1:T(4,128)(2,1)} %get-tuple-element.257), channel_id=1, source_target_pairs={{0,4},{4,8},{8,12},{12,16},{16,20},{20,24},{24,28},{28,32},{32,36}... | collective-permute-start | bytes 98312 | tf_op jit(solution)/shard_map/ppermute | solution.py:12
  208.6 58.6 %collective-permute-start.26 = (bf16[4,32,128]{2,0,1:T(4,128)(2,1)}, bf16[4,32,128]{2,0,1:T(4,128)(2,1)}, u32[]{:S(2)}, u32[]{:S(2)}) collective-permute-start(bf16[4,32,128]{2,0,1:T(4,128)(2,1)} %get-tuple-element.263), channel_id=1, source_target_pairs={{0,8},{4,12},{8,16},{12,20},{16,24},{20,28},{24,32},{28,36},{32,40... | collective-permute-start | bytes 98312 | tf_op jit(solution)/shard_map/ppermute | solution.py:12
  214.8 67.3 %collective-permute-start.27 = (bf16[4,32,128]{2,0,1:T(4,128)(2,1)}, bf16[4,32,128]{2,0,1:T(4,128)(2,1)}, u32[]{:S(2)}, u32[]{:S(2)}) collective-permute-start(bf16[4,32,128]{2,0,1:T(4,128)(2,1)} %get-tuple-element.262), channel_id=1, source_target_pairs={{0,12},{4,16},{8,20},{12,24},{16,28},{20,32},{24,36},{28,40},{32,4... | collective-permute-start | bytes 98312 | tf_op jit(solution)/shard_map/ppermute | solution.py:12
  220.5 61.7 %collective-permute-start.28 = (bf16[4,32,128]{2,0,1:T(4,128)(2,1)}, bf16[4,32,128]{2,0,1:T(4,128)(2,1)}, u32[]{:S(2)}, u32[]{:S(2)}) collective-permute-start(bf16[4,32,128]{2,0,1:T(4,128)(2,1)} %get-tuple-element.261), channel_id=1, source_target_pairs={{0,16},{4,20},{8,24},{12,28},{16,32},{20,36},{24,40},{28,44},{32,4... | collective-permute-start | bytes 98312 | tf_op jit(solution)/shard_map/ppermute | solution.py:12
  262.7 15.7 %collective-permute-start.17 = (bf16[4,128,256]{2,1,0:T(8,128)(2,1)S(1)}, bf16[4,128,256]{2,1,0:T(8,128)(2,1)S(1)}, u32[]{:S(2)}, u32[]{:S(2)}) collective-permute-start(bf16[4,128,256]{2,1,0:T(8,128)(2,1)S(1)} %slice.134), channel_id=1, source_target_pairs={{0,4},{4,8},{8,12},{12,16},{16,20},{20,24},{24,28},{28,32},{32,36}... | collective-permute-start | bytes 786440 | tf_op jit(solution)/shard_map/ppermute | solution.py:12
  265.8 16.3 %collective-permute-start.29 = (bf16[4,32,128]{2,0,1:T(4,128)(2,1)S(1)}, bf16[4,32,128]{2,0,1:T(4,128)(2,1)S(1)}, u32[]{:S(2)}, u32[]{:S(2)}) collective-permute-start(bf16[4,32,128]{2,0,1:T(4,128)(2,1)S(1)} %copy-done.13), channel_id=1, source_target_pairs={{0,20},{4,24},{8,28},{12,32},{16,36},{20,40},{24,44},{28,48},{32,5... | collective-permute-start | bytes 98312 | tf_op jit(solution)/shard_map/ppermute | solution.py:12
  267.2 15.0 %collective-permute-start.30 = (bf16[4,32,128]{2,0,1:T(4,128)(2,1)S(1)}, bf16[4,32,128]{2,0,1:T(4,128)(2,1)S(1)}, u32[]{:S(2)}, u32[]{:S(2)}) collective-permute-start(bf16[4,32,128]{2,0,1:T(4,128)(2,1)S(1)} %copy-done.12), channel_id=1, source_target_pairs={{0,24},{4,28},{8,32},{12,36},{16,40},{20,44},{24,48},{28,52},{32,5... | collective-permute-start | bytes 98312 | tf_op jit(solution)/shard_map/ppermute | solution.py:12
  (28 other events, 328.3 us)
Sparse Core Ops, SparseCore 0:
  122.6 58.3 all-reduce.2
  282.3 63.7 all-reduce.4
where the time goes:
time: 359 us; the launch traced here: 355 us
  starting transfers between devices  114 us (32%)
  waiting for transfers between devices  91.1 us (25%)
  matrix products  45.9 us (13%)
  local copies, waits for them, and re-layouts  44.1 us (12%)
  blocking collectives  28.2 us (8%)
  between operations  16.2 us (5%)
  other arithmetic  15.1 us (4%)
    ppermute x32, starting transfers between devices, shifted(): return lax.ppermute(x, axis, pairs)  114 us
    psum x2, waiting for transfers between devices, apply_operator(): lax.psum(own_near.astype(jnp.bfloat16), 'col').astype(jnp.float32)  91 us
    psum x2, blocking collectives, apply_operator(): lax.psum(far_total.astype(jnp.bfloat16), 'col').astype(jnp.float32)  28.2 us
    dot_general x20, matrix products, hot_sum(): jnp.einsum(form, hot_table, lower, preferred_element_type=jnp.float32)  25.7 us
    gather x8, local copies, waits for them, and re-layouts, one_group(): col_field = jnp.take(window_field, col_ids, axis=0)  12.8 us
    gather x8, local copies, waits for them, and re-layouts, one_group(): row_field = jnp.take(window_field, row_ids, axis=0)  12.8 us
    unnamed x66, local copies, waits for them, and re-layouts  8.37 us
    dot_general x20, matrix products, hot_sum(): jnp.einsum(form, hot_table, upper, preferred_element_type=jnp.float32)  7.55 us
  transfers between devices with their start and end apart: 34, of which 2 were waited for; matrix products, arithmetic and copies ran while one was open for 28% of the time, Pallas kernels for 0%

commit v1 on v0

v1 whole, which is shorter than its diff:
```python
import functools

import jax
import jax.numpy as jnp
from jax import lax
from jax.experimental import pallas as pl
from jax.experimental.pallas import tpu as pltpu
from jax.sharding import PartitionSpec as P

MESH = pl.DeviceIdType.MESH
F32 = jnp.float32
BF16 = jnp.bfloat16
I32 = jnp.int32

SLAB = 4
REACH = 7
NEAR = 16
FAR = 128
RANK = 32
RHS = 128
PANELS = 256
LANES = 128

FIELD, COEF, AHEAD, PART, FARPART, FARBACK, IMAGE, PER_APPLY = 0, 4, 11, 15, 18, 21, 28, 31
DENSE = 2 * PER_APPLY
N_SEMS = DENSE + 3


def sort_keys(unique_keys):
    across = jnp.broadcast_to(unique_keys, (LANES, LANES))
    down = across.T
    rank = jnp.sum(jnp.where(across < down, 1, 0).astype(I32), axis=1, keepdims=True)
    lane = lax.broadcasted_iota(I32, (LANES, LANES), 1)
    ordered = jnp.sum(jnp.where(rank == lane, down, 0), axis=0, keepdims=True)
    return ordered, down


def count_upto(down, shift):
    lane = lax.broadcasted_iota(I32, (LANES, LANES), 1)
    return jnp.sum(jnp.where((down >> shift) <= lane, 1, 0).astype(I32), axis=0, keepdims=True)


def kernel(
    n_rows,
    charges_hbm,
    basis_ref,
    sizes_ref,
    blocks_hbm,
    near_rows_ref,
    near_cols_ref,
    near_live_ref,
    couplings_hbm,
    far_rows_ref,
    far_cols_ref,
    far_live_ref,
    out1_hbm,
    out2_hbm,
    charges,
    blocks,
    couplings,
    own_first,
    own_second,
    next_first,
    next_second,
    final,
    order_v,
    order_s,
    coef_own,
    coef_ahead,
    spread,
    far_prefix,
    dense_send,
    dense_recv,
    dense,
    near_prefix,
    back_prefix,
    ahead_send,
    ahead_recv,
    part_send,
    part_recv,
    farpart_send,
    farpart_recv,
    farback_send,
    farback_recv,
    send_sem,
    recv_sem,
    load_sem,
):
    r = lax.axis_index("row")
    c = lax.axis_index("col")
    own = (own_first, own_second)
    ahead = (next_first, next_second)

    def up(o):
        return (lax.rem(r + o, n_rows), c)

    def down(o):
        return (lax.rem(r + n_rows - o, n_rows), c)

    def beside(d):
        return (r, lax.rem(c + d, SLAB))

    def remote(src, dst, at, device):
        return pltpu.make_async_remote_copy(
            src_ref=src,
            dst_ref=dst,
            send_sem=send_sem.at[at],
            recv_sem=recv_sem.at[at],
            device_id=device,
            device_id_type=MESH,
        )

    load_charges = pltpu.make_async_copy(charges_hbm, charges, load_sem.at[0])
    load_couplings = pltpu.make_async_copy(couplings_hbm, couplings, load_sem.at[1])
    load_blocks = pltpu.make_async_copy(blocks_hbm, blocks, load_sem.at[2])
    load_charges.start()
    load_couplings.start()
    load_blocks.start()

    barrier = pltpu.get_barrier_semaphore()
    peers = [up(o) for o in range(1, REACH + 1)]
    peers += [down(o) for o in range(1, REACH + 1)]
    peers += [beside(d) for d in range(1, SLAB)]
    for peer in peers:
        pl.semaphore_signal(barrier, inc=1, device_id=peer, device_id_type=MESH)

    first = r * SLAB
    lane = lax.broadcasted_iota(I32, (1, LANES), 1)
    near_used = near_live_ref[0]
    by_row = jnp.broadcast_to((1 << 16) + lane, (1, LANES))
    by_col = by_row
    for s in range(NEAR):
        row = jnp.clip(near_rows_ref[s] - first, 0, SLAB - 1)
        col = jnp.clip(near_cols_ref[s] - first, 0, 2 * SLAB - 1)
        used = s < near_used
        row_key = (jnp.where(used, row, SLAB) << 7) + (col << 4) + s
        col_key = (jnp.where(used, col, 2 * SLAB) << 7) + (row << 4) + s
        by_row = jnp.where(lane == s, row_key, by_row)
        by_col = jnp.where(lane == s, col_key, by_col)
    far_row = jnp.clip(far_rows_ref[...] - first, 0, SLAB - 1).reshape(1, LANES)
    far_col = jnp.clip(far_cols_ref[...] - first - SLAB, 0, REACH * SLAB - 1).reshape(1, LANES)
    far_slab = far_col >> 2
    far_group = ((far_col & 3) * SLAB + far_row) * 2 + (far_slab >> 2)
    far_group = jnp.where(lane < far_live_ref[0], far_group, 2 * SLAB * SLAB)
    by_tile = ((far_group * 4 + (far_slab & 3)) << 7) + lane
    for at, (keys, shift) in enumerate(((by_row, 7), (by_col, 7), (by_tile, 9))):
        ordered, laid = sort_keys(keys)
        order_v[2 * at : 2 * at + 1, :] = ordered
        order_v[2 * at + 1 : 2 * at + 2, :] = count_upto(laid, shift)
    order_v[6:8, :] = jnp.zeros((2, LANES), I32)
    share_order = pltpu.make_async_copy(order_v, order_s, load_sem.at[3])
    share_order.start()

    panel = lax.broadcasted_iota(I32, (RHS, PANELS), 1)

    def masked(values, size):
        return jnp.where(panel < size, values, jnp.zeros_like(values))

    def last_of(row, group):
        upto = order_s[row, group]
        before = order_s[row, group - 1] if group > 0 else 0
        return jnp.maximum(upto - 1, 0), (upto > before).astype(F32)

    def coefficients(a, i):
        return lax.dot_general(
            basis_ref[i], own[a][i], (((1,), (1,)), ((), ())), preferred_element_type=F32
        ).astype(BF16)

    def own_coefficients(a):
        for i in range(SLAB):
            coef_own[a, i * RANK : (i + 1) * RANK, :] = coefficients(a, i)

    def near_pass(a, order_row, forward, prefix):
        def slot(k, carry):
            total, previous = carry
            key = order_s[order_row, k]
            group = key >> 7
            other = (key >> 4) & 7
            source = own[a][other & 3]
            if forward:
                source = jnp.where(other < SLAB, source, ahead[a][other & 3])
            block = blocks[key & 15]
            product = lax.dot_general(
                source,
                block,
                (((1,), (1 if forward else 0,)), ((), ())),
                preferred_element_type=F32,
            )
            total = total * (group == previous).astype(F32) + product
            prefix[k] = total
            return total, group

        lax.fori_loop(0, NEAR, slot, (jnp.zeros((RHS, PANELS), F32), jnp.int32(-1)))

    def send_coefficients(a):
        copies = []
        mine = coef_own.at[a, pl.ds(pl.multiple_of(c * RANK, RANK), RANK), :]
        for o in range(1, REACH + 1):
            copy = remote(
                mine,
                coef_ahead.at[a, (o - 1) * RANK : o * RANK, :],
                a * PER_APPLY + COEF + o - 1,
                down(o),
            )
            copy.start()
            copies.append(copy)
        return copies

    sent = []
    for a in range(2):
        coef_ahead[a, REACH * RANK :, :] = jnp.zeros((RANK, RHS), BF16)
    load_charges.wait()
    for i in range(SLAB):
        own_first[i] = masked(charges[i], sizes_ref[i])
    own_coefficients(0)

    pl.semaphore_wait(barrier, len(peers))

    field_copies = [
        remote(own_first.at[i], next_first.at[i], FIELD + i, down(1)) for i in range(SLAB)
    ]
    for copy in field_copies:
        copy.start()
    coef_copies = send_coefficients(0)

    load_couplings.wait()
    share_order.wait()
    rank_at = lax.broadcasted_iota(I32, (RANK, LANES), 0)
    lane_at = lax.broadcasted_iota(I32, (RANK, LANES), 1)
    repeat = jnp.where((lane_at & (RANK - 1)) == rank_at, 1.0, 0.0).astype(BF16)

    def spread_some(n, _):
        some = couplings[pl.ds(n * 16, 16)].reshape(16 * RANK, RANK)
        spread[pl.ds(n * 16, 16)] = jnp.dot(
            some, repeat, preferred_element_type=F32
        ).reshape(16, RANK, LANES)
        return 0

    lax.fori_loop(0, FAR // 16, spread_some, 0)

    def far_slot(k, carry):
        total, previous = carry
        key = order_s[4, k]
        group = key >> 9
        kept = jnp.where((lane_at >> 5) == ((key >> 7) & 3), spread[key & 127], 0.0)
        total = total * (group == previous).astype(F32) + kept
        far_prefix[k] = total
        return total, group

    lax.fori_loop(0, FAR, far_slot, (jnp.zeros((RANK, LANES), F32), jnp.int32(-1)))
    for g in range(2 * SLAB * SLAB):
        at, live = last_of(5, g)
        i, half = (g // 2) % SLAB, g % 2
        dense_send[
            g // (2 * SLAB), i * RANK : (i + 1) * RANK, half * LANES : (half + 1) * LANES
        ] = (far_prefix[at] * live).astype(BF16)
    dense_copies = []
    for d in (2, 1, 3):
        copy = remote(
            dense_send.at[lax.rem(c + d, SLAB)], dense_recv.at[d - 1], DENSE + d - 1, beside(d)
        )
        copy.start()
        dense_copies.append(copy)

    load_blocks.wait()

    for a in range(2):
        base = a * PER_APPLY
        near_pass(a, 2, False, back_prefix)
        for j in range(SLAB):
            at, live = last_of(3, SLAB + j)
            ahead_send[a, j] = (back_prefix[at] * live).astype(BF16)
        ahead_copies = [
            remote(ahead_send.at[a, j], ahead_recv.at[a, j], base + AHEAD + j, up(1))
            for j in range(SLAB)
        ]
        for copy in ahead_copies:
            copy.start()

        if a == 0:
            for copy in dense_copies:
                copy.wait_recv()
            total = dense_send[c].astype(F32)
            for d in range(SLAB - 1):
                total = total + dense_recv[d].astype(F32)
            dense[...] = total.astype(BF16)
        back = lax.dot_general(
            dense[...], coef_own[a], (((0,), (0,)), ((), ())), preferred_element_type=F32
        )
        farback_send[a] = back.astype(BF16)
        farback_copies = []
        for o in range(1, REACH + 1):
            copy = remote(
                farback_send.at[a, (o - 1) * RANK : o * RANK, :],
                farback_recv.at[a, o - 1],
                base + FARBACK + o - 1,
                up(o),
            )
            copy.start()
            farback_copies.append(copy)
        for copy in coef_copies:
            copy.wait_recv()
        farpart_send[a] = jnp.dot(
            dense[...], coef_ahead[a], preferred_element_type=F32
        ).astype(BF16)
        farpart_copies = []
        for d in (2, 1, 3):
            other = lax.rem(c + d, SLAB)
            copy = remote(
                farpart_send.at[a, pl.ds(pl.multiple_of(other * RANK, RANK), RANK), :],
                farpart_recv.at[a, d - 1],
                base + FARPART + d - 1,
                beside(d),
            )
            copy.start()
            farpart_copies.append(copy)

        for copy in field_copies:
            copy.wait_recv()
        near_pass(a, 0, True, near_prefix)
        for copy in ahead_copies:
            copy.wait_recv()

        def own_near(i):
            upto = order_s[1, i]
            before = jnp.where(i > 0, order_s[1, jnp.maximum(i - 1, 0)], 0)
            forward = near_prefix[jnp.maximum(upto - 1, 0)] * (upto > before).astype(F32)
            upto = order_s[3, i]
            before = jnp.where(i > 0, order_s[3, jnp.maximum(i - 1, 0)], 0)
            backward = back_prefix[jnp.maximum(upto - 1, 0)] * (upto > before).astype(F32)
            return forward + backward + ahead_recv[a, i].astype(F32)

        part_copies = []
        for d in (2, 1, 3):
            part_send[a, d - 1] = own_near(lax.rem(c + d, SLAB)).astype(BF16)
            copy = remote(
                part_send.at[a, d - 1], part_recv.at[a, d - 1], base + PART + d - 1, beside(d)
            )
            copy.start()
            part_copies.append(copy)
        image = own_near(c)

        for copy in farpart_copies + farback_copies:
            copy.wait_recv()
        far_total = farpart_send[a, pl.ds(pl.multiple_of(c * RANK, RANK), RANK), :].astype(F32)
        for d in range(SLAB - 1):
            far_total = far_total + farpart_recv[a, d].astype(F32)
        for o in range(REACH):
            far_total = far_total + farback_recv[a, o].astype(F32)
        image = image + lax.dot_general(
            far_total.astype(BF16),
            basis_ref[c],
            (((0,), (0,)), ((), ())),
            preferred_element_type=F32,
        )
        for copy in part_copies:
            copy.wait_recv()
        for d in range(SLAB - 1):
            image = image + part_recv[a, d].astype(F32)
        image = masked(image, sizes_ref[c]).astype(BF16)

        target = own_second if a == 0 else final
        target[c] = image
        image_copies = []
        for d in (2, 1, 3):
            copy = remote(target.at[c], target.at[c], base + IMAGE + d - 1, beside(d))
            copy.start()
            image_copies.append(copy)
        sent += ahead_copies + farback_copies + farpart_copies + part_copies + image_copies
        sent += field_copies + coef_copies
        if a == 0:
            coef_own[1, pl.ds(pl.multiple_of(c * RANK, RANK), RANK), :] = coefficients(1, c)
            relay = remote(own_second.at[c], next_second.at[c], PER_APPLY + FIELD, down(1))
            relay.start()
            field_copies = [relay]
            coef_copies = send_coefficients(1)
            for at, d in ((1, 1), (2, 3), (0, 2)):
                image_copies[at].wait_recv()
                source = lax.rem(c + SLAB - d, SLAB)
                relay = remote(
                    own_second.at[source], next_second.at[source], PER_APPLY + FIELD + d, down(1)
                )
                relay.start()
                field_copies.append(relay)
                coef_own[1, pl.ds(pl.multiple_of(source * RANK, RANK), RANK), :] = coefficients(
                    1, source
                )
            store_first = pltpu.make_async_copy(own_second, out1_hbm, load_sem.at[4])
            store_first.start()
        else:
            for copy in image_copies:
                copy.wait_recv()
            store_second = pltpu.make_async_copy(final, out2_hbm, load_sem.at[5])
            store_second.start()
    for copy in sent + dense_copies:
        copy.wait_send()
    store_first.wait()
    store_second.wait()


def per_device(n_rows, *arrays):
    smem = pl.BlockSpec(memory_space=pltpu.SMEM)
    vmem = pl.BlockSpec(memory_space=pltpu.VMEM)
    hbm = pl.BlockSpec(memory_space=pl.ANY)
    image = jax.ShapeDtypeStruct((SLAB, RHS, PANELS), BF16)
    return pl.pallas_call(
        functools.partial(kernel, n_rows),
        out_shape=(image, image),
        in_specs=[hbm, vmem, smem, hbm, smem, smem, smem, hbm, vmem, vmem, smem],
        out_specs=(hbm, hbm),
        scratch_shapes=[
            pltpu.VMEM((SLAB, RHS, PANELS), BF16),
            pltpu.VMEM((NEAR, PANELS, PANELS), BF16),
            pltpu.VMEM((FAR, RANK, RANK), BF16),
            pltpu.VMEM((SLAB, RHS, PANELS), BF16),
            pltpu.VMEM((SLAB, RHS, PANELS), BF16),
            pltpu.VMEM((SLAB, RHS, PANELS), BF16),
            pltpu.VMEM((SLAB, RHS, PANELS), BF16),
            pltpu.VMEM((SLAB, RHS, PANELS), BF16),
            pltpu.VMEM((8, LANES), I32),
            pltpu.SMEM((8, LANES), I32),
            pltpu.VMEM((2, SLAB * RANK, RHS), BF16),
            pltpu.VMEM((2, (REACH + 1) * RANK, RHS), BF16),
            pltpu.VMEM((FAR, RANK, LANES), F32),
            pltpu.VMEM((FAR, RANK, LANES), F32),
            pltpu.VMEM((SLAB, SLAB * RANK, 2 * LANES), BF16),
            pltpu.VMEM((SLAB - 1, SLAB * RANK, 2 * LANES), BF16),
            pltpu.VMEM((SLAB * RANK, 2 * LANES), BF16),
            pltpu.VMEM((NEAR, RHS, PANELS), F32),
            pltpu.VMEM((NEAR, RHS, PANELS), F32),
            pltpu.VMEM((2, SLAB, RHS, PANELS), BF16),
            pltpu.VMEM((2, SLAB, RHS, PANELS), BF16),
            pltpu.VMEM((2, SLAB - 1, RHS, PANELS), BF16),
            pltpu.VMEM((2, SLAB - 1, RHS, PANELS), BF16),
            pltpu.VMEM((2, SLAB * RANK, RHS), BF16),
            pltpu.VMEM((2, SLAB - 1, RANK, RHS), BF16),
            pltpu.VMEM((2, (REACH + 1) * RANK, RHS), BF16),
            pltpu.VMEM((2, REACH, RANK, RHS), BF16),
            pltpu.SemaphoreType.DMA((N_SEMS,)),
            pltpu.SemaphoreType.DMA((N_SEMS,)),
            pltpu.SemaphoreType.DMA((6,)),
        ],
        compiler_params=pltpu.CompilerParams(
            collective_id=0, has_side_effects=True, vmem_limit_bytes=40 * 1024 * 1024
        ),
    )(*arrays)


def solution(mesh):
    placed = (
        P("row", None, None),
        P("row", None, None),
        P("row"),
        P(("row", "col"), None, None),
        P(("row", "col")),
        P(("row", "col")),
        P(("row", "col")),
        P(("row", "col"), None, None),
        P(("row", "col")),
        P(("row", "col")),
        P(("row", "col")),
    )
    return jax.shard_map(
        functools.partial(per_device, mesh.shape["row"]),
        mesh=mesh,
        in_specs=placed,
        out_specs=(P("row", None, None), P("row", None, None)),
        check_vma=False,
    )
```

time: 359 us -> 74.1 us (0.21)
  the two profiles are of different devices: /device:TPU:1 before, /device:TPU:2 now
where the time goes in v1:
time: 74.1 us; the launch traced here: 73.7 us
  Pallas kernels  61.3 us (83%)
  local copies, waits for them, and re-layouts  10.4 us (14%)
  between operations  1.95 us (3%)
    pallas_call x1, Pallas kernels, per_device(): pl.pallas_call(functools.partial(kernel, n_rows), out_shape=(image, image...  61.3 us
    unnamed x19, local copies, waits for them, and re-layouts  10.4 us

profile of v1, /device:TPU:2, one launch (start us, length us, event | category | flops | bytes accessed | tf_op | source)
XLA Modules:
  0.0 73.7 jit_solution(16018397469472943212)
XLA Ops:
  1.9 2.4 %copy.13.couplings_hbm = bf16[128,32,32]{2,1,0:T(8,128)(2,1)S(1)} copy(bf16[128,32,32]{0,2,1:T(8,128)(2,1)} %param.18) | data formatting | bytes 524288 | tf_op args[7]
  4.3 0.0 copy-start
  4.3 1.6 %copy-done = bf16[16,256,256]{2,1,0:T(8,128)(2,1)S(1)} copy-done((bf16[16,256,256]{2,1,0:T(8,128)(2,1)S(1)}, bf16[16,256,256]{2,1,0:T(8,128)(2,1)}, u32[]{:S(2)}) %copy-start) | copy-done | bytes 2097176
  5.9 0.0 copy-start.1
  5.9 0.9 %copy-done.1 = bf16[4,128,256]{2,1,0:T(8,128)(2,1)S(1)} copy-done((bf16[4,128,256]{2,1,0:T(8,128)(2,1)S(1)}, bf16[4,128,256]{2,1,0:T(8,128)(2,1)}, u32[]{:S(2)}) %copy-start.1) | copy-done | bytes 262168
  6.9 0.0 copy-start.2
  6.9 0.8 %copy-done.2 = bf16[4,32,256]{2,1,0:T(8,128)(2,1)S(1)} copy-done((bf16[4,32,256]{2,1,0:T(8,128)(2,1)S(1)}, bf16[4,32,256]{2,1,0:T(8,128)(2,1)}, u32[]{:S(2)}) %copy-start.2) | copy-done | bytes 65560
  7.7 0.0 copy-start.3
  7.7 0.7 copy-done.3
  8.3 0.0 copy-start.4
  8.3 0.7 copy-done.4
  9.0 0.0 copy-start.5
  9.0 0.7 copy-done.5
  9.7 0.0 copy-start.6
  9.7 0.7 copy-done.6
  10.3 0.0 copy-start.7
  10.3 0.7 copy-done.7
  11.0 61.3 %shard_map.122 = (bf16[4,128,256]{2,1,0:T(8,128)(2,1)S(1)}, bf16[4,128,256]{2,1,0:T(8,128)(2,1)S(1)}) custom-call(bf16[4,128,256]{2,1,0:T(8,128)(2,1)S(1)} %copy-done.1, bf16[4,32,256]{2,1,0:T(8,128)(2,1)S(1)} %copy-done.2, s32[4]{0:T(128)S(1)} %copy-done.3, bf16[16,256,256]{2,1,0:T(8,128)(2,1)S(1)} %copy-done, s32[16]{0:T(128)S(1)} %copy-done.4, ...), custom_call_target="tpu_custom_call" | custom-call | tf_op jit(solution)/shard_map/pallas_call | solution.py:406
  72.3 0.7 copy.18
  73.0 0.7 copy.19
Async XLA Ops:
  4.3 1.6 %copy-start = (bf16[16,256,256]{2,1,0:T(8,128)(2,1)S(1)}, bf16[16,256,256]{2,1,0:T(8,128)(2,1)}, u32[]{:S(2)}) copy-start(bf16[16,256,256]{2,1,0:T(8,128)(2,1)} %blocks_hbm.1) | copy-start | bytes 6291460
  5.9 0.9 %copy-start.1 = (bf16[4,128,256]{2,1,0:T(8,128)(2,1)S(1)}, bf16[4,128,256]{2,1,0:T(8,128)(2,1)}, u32[]{:S(2)}) copy-start(bf16[4,128,256]{2,1,0:T(8,128)(2,1)} %charges_hbm.1) | copy-start | bytes 786436
  6.9 0.8 %copy-start.2 = (bf16[4,32,256]{2,1,0:T(8,128)(2,1)S(1)}, bf16[4,32,256]{2,1,0:T(8,128)(2,1)}, u32[]{:S(2)}) copy-start(bf16[4,32,256]{2,1,0:T(8,128)(2,1)} %basis_ref.1) | copy-start | bytes 196612
  7.7 0.7 copy-start.3
  8.3 0.7 copy-start.4
  9.0 0.7 copy-start.5
  9.7 0.7 copy-start.6
  10.3 0.7 copy-start.7

commit v2 on v1

v2 whole, which is shorter than its diff:
```python
import functools

import jax
import jax.numpy as jnp
from jax import lax
from jax.experimental import pallas as pl
from jax.experimental.pallas import tpu as pltpu
from jax.sharding import PartitionSpec as P

MESH = pl.DeviceIdType.MESH
F32 = jnp.float32
BF16 = jnp.bfloat16
I32 = jnp.int32

SLAB = 4
REACH = 7
NEAR = 16
FAR = 128
RANK = 32
RHS = 128
PANELS = 256
LANES = 128
UNROLL = 8

FIELD, COEF, AHEAD, PART, FARPART, FARBACK, IMAGE, PER_APPLY = 0, 4, 11, 15, 18, 21, 28, 31
DENSE = 2 * PER_APPLY
N_SEMS = DENSE + 3
TURNS = (2, 1, 3, 0)


def sort_keys(unique_keys):
    across = jnp.broadcast_to(unique_keys, (LANES, LANES))
    down = across.T
    rank = jnp.sum(jnp.where(across < down, 1, 0).astype(I32), axis=1, keepdims=True)
    lane = lax.broadcasted_iota(I32, (LANES, LANES), 1)
    ordered = jnp.sum(jnp.where(rank == lane, down, 0), axis=0, keepdims=True)
    return ordered, down


def count_upto(down, shift):
    lane = lax.broadcasted_iota(I32, (LANES, LANES), 1)
    return jnp.sum(jnp.where((down >> shift) <= lane, 1, 0).astype(I32), axis=0, keepdims=True)


def kernel(
    n_rows,
    charges_hbm,
    basis_hbm,
    sizes_hbm,
    blocks_hbm,
    near_rows_hbm,
    near_cols_hbm,
    near_live_hbm,
    couplings_hbm,
    far_rows_hbm,
    far_cols_hbm,
    far_live_hbm,
    first_image,
    second_image,
    charges,
    basis_ref,
    sizes_ref,
    blocks,
    near_rows_ref,
    near_cols_ref,
    near_live_ref,
    couplings,
    far_rows_ref,
    far_cols_ref,
    far_live_ref,
    masked_charges,
    next_first,
    next_second,
    order_v,
    order_s,
    coef_own,
    coef_ahead,
    dense_sum,
    dense_send,
    dense_recv,
    dense,
    near_prefix,
    back_prefix,
    ahead_send,
    ahead_recv,
    part_send,
    part_recv,
    farpart_send,
    farpart_recv,
    farback_send,
    farback_recv,
    send_sem,
    recv_sem,
    load_sem,
):
    r = lax.axis_index("row")
    c = lax.axis_index("col")
    own = (masked_charges, first_image)
    ahead = (next_first, next_second)
    images = (first_image, second_image)
    rows_above = jnp.minimum(REACH, n_rows - 1 - r)
    rows_below = jnp.minimum(REACH, r)
    has_above = r < n_rows - 1
    has_below = r > 0

    def up(o):
        return (lax.rem(r + o, n_rows), c)

    def down(o):
        return (lax.rem(r + n_rows - o, n_rows), c)

    def beside(d):
        return (r, lax.rem(c + d, SLAB))

    def cluster(turn):
        return lax.rem(c + turn, SLAB)

    def ranks(i):
        return pl.ds(pl.multiple_of(i * RANK, RANK), RANK)

    def remote(src, dst, at, device):
        return pltpu.make_async_remote_copy(
            src_ref=src,
            dst_ref=dst,
            send_sem=send_sem.at[at],
            recv_sem=recv_sem.at[at],
            device_id=device,
            device_id_type=MESH,
        )

    def field_copy(a, turn):
        i = cluster(SLAB - turn)
        return remote(own[a].at[i], ahead[a].at[i], a * PER_APPLY + FIELD + turn, down(1))

    def coef_copy(a, o):
        return remote(
            coef_own.at[a, ranks(c), :],
            coef_ahead.at[a, ranks(o - 1), :],
            a * PER_APPLY + COEF + o - 1,
            down(o),
        )

    def ahead_copy(a, turn):
        return remote(
            ahead_send.at[a, turn], ahead_recv.at[a, turn], a * PER_APPLY + AHEAD + turn, up(1)
        )

    def part_copy(a, d):
        return remote(
            part_send.at[a, d - 1], part_recv.at[a, d - 1], a * PER_APPLY + PART + d - 1, beside(d)
        )

    def farpart_copy(a, d):
        return remote(
            farpart_send.at[a, ranks(cluster(d)), :],
            farpart_recv.at[a, d - 1],
            a * PER_APPLY + FARPART + d - 1,
            beside(d),
        )

    def farback_copy(a, o):
        return remote(
            farback_send.at[a, ranks(o - 1), :],
            farback_recv.at[a, o - 1],
            a * PER_APPLY + FARBACK + o - 1,
            up(o),
        )

    def image_copy(a, d):
        return remote(
            images[a].at[c], images[a].at[c], a * PER_APPLY + IMAGE + d - 1, beside(d)
        )

    def dense_copy(d):
        return remote(
            dense_send.at[cluster(d)], dense_recv.at[d - 1], DENSE + d - 1, beside(d)
        )

    def each(count, act):
        def step(o, _):
            act(o)
            return 0

        lax.fori_loop(1, count + 1, step, 0)

    loads = [
        pltpu.make_async_copy(source, target, load_sem.at[at])
        for at, (source, target) in enumerate(
            (
                (charges_hbm, charges),
                (sizes_hbm, sizes_ref),
                (basis_hbm, basis_ref),
                (near_rows_hbm, near_rows_ref),
                (near_cols_hbm, near_cols_ref),
                (near_live_hbm, near_live_ref),
                (far_rows_hbm, far_rows_ref),
                (far_cols_hbm, far_cols_ref),
                (far_live_hbm, far_live_ref),
                (couplings_hbm, couplings),
                (blocks_hbm, blocks),
            )
        )
    ]
    for load in loads:
        load.start()

    coef_ahead[...] = jnp.zeros_like(coef_ahead)
    farback_recv[...] = jnp.zeros_like(farback_recv)

    @pl.when(jnp.logical_not(has_above))
    def _():
        next_first[...] = jnp.zeros_like(next_first)
        next_second[...] = jnp.zeros_like(next_second)

    @pl.when(jnp.logical_not(has_below))
    def _():
        ahead_recv[...] = jnp.zeros_like(ahead_recv)

    barrier = pltpu.get_barrier_semaphore()

    def greet(device):
        pl.semaphore_signal(barrier, inc=1, device_id=device, device_id_type=MESH)

    for d in range(1, SLAB):
        greet(beside(d))
    each(rows_above, lambda o: greet(up(o)))
    each(rows_below, lambda o: greet(down(o)))

    panel = lax.broadcasted_iota(I32, (RHS, PANELS), 1)

    def masked(values, size):
        return jnp.where(panel < size, values, jnp.zeros_like(values))

    def last_of(row, group):
        upto = order_s[row, group]
        before = jnp.where(group > 0, order_s[row, jnp.maximum(group - 1, 0)], 0)
        return jnp.maximum(upto - 1, 0), (upto > before).astype(F32)

    def set_coefficients(a, i):
        coef_own[a, ranks(i), :] = lax.dot_general(
            basis_ref[i], own[a][i], (((1,), (1,)), ((), ())), preferred_element_type=F32
        ).astype(BF16)

    def near_pass(a, order_row, forward, prefix):
        def slot(k, carry):
            total, previous = carry
            key = order_s[order_row, k]
            group = key >> 7
            other = (key >> 4) & 7
            source = own[a][other & 3]
            if forward:
                source = jnp.where(other < SLAB, source, ahead[a][other & 3])
            block = blocks[key & 15]
            product = lax.dot_general(
                source,
                block,
                (((1,), (1 if forward else 0,)), ((), ())),
                preferred_element_type=F32,
            )
            total = total * (group == previous).astype(F32) + product
            prefix[k] = total
            return total, group

        start = (jnp.zeros((RHS, PANELS), F32), jnp.int32(-1))
        lax.fori_loop(0, NEAR, slot, start, unroll=UNROLL)

    for load in loads[0:3]:
        load.wait()
    for i in range(SLAB):
        masked_charges[i] = masked(charges[i], sizes_ref[i])
    set_coefficients(0, c)

    pl.semaphore_wait(barrier, SLAB - 1 + rows_above + rows_below)

    @pl.when(has_below)
    def _():
        for turn in range(SLAB):
            field_copy(0, turn).start()

    each(rows_below, lambda o: coef_copy(0, o).start())

    for load in loads[3:9]:
        load.wait()
    first = r * SLAB
    lane = lax.broadcasted_iota(I32, (1, LANES), 1)
    near_used = near_live_ref[0]
    by_row = jnp.broadcast_to((1 << 16) + lane, (1, LANES))
    by_col = by_row
    for s in range(NEAR):
        row = jnp.clip(near_rows_ref[s] - first, 0, SLAB - 1)
        col = jnp.clip(near_cols_ref[s] - first, 0, 2 * SLAB - 1)
        used = s < near_used
        row_key = (jnp.where(used, row, SLAB) << 7) + (col << 4) + s
        col_key = (jnp.where(used, col, 2 * SLAB) << 7) + (row << 4) + s
        by_row = jnp.where(lane == s, row_key, by_row)
        by_col = jnp.where(lane == s, col_key, by_col)
    for at, keys in enumerate((by_row, by_col)):
        ordered, laid = sort_keys(keys)
        order_v[2 * at : 2 * at + 1, :] = ordered
        order_v[2 * at + 1 : 2 * at + 2, :] = count_upto(laid, 7)
    order_v[4:8, :] = jnp.zeros((4, LANES), I32)
    share_order = pltpu.make_async_copy(order_v, order_s, load_sem.at[11])
    share_order.start()

    far_row = jnp.clip(far_rows_ref[...] - first, 0, SLAB - 1).reshape(1, LANES)
    far_col = jnp.clip(far_cols_ref[...] - first - SLAB, 0, REACH * SLAB - 1).reshape(1, LANES)
    far_slab = far_col >> 2
    far_key = (far_col & 3) * (2 * SLAB) + far_row
    far_key = jnp.where(lane < far_live_ref[0], far_key, -2 * SLAB)
    loads[9].wait()
    target = lax.broadcasted_iota(I32, (8 * SLAB, 2 * LANES), 0)
    chosen = jnp.where(target == jnp.concatenate([far_key, far_key + SLAB], axis=1), 1.0, 0.0)
    chosen = chosen.astype(BF16)
    in_slab = [
        jnp.broadcast_to(jnp.where(far_slab == o, 1.0, 0.0), (RANK, LANES)).astype(BF16)
        for o in range(REACH)
    ]

    def dense_rows(m, _):
        halves = []
        for half in range(2):
            block = couplings[2 * m + half]
            tiles = [block * in_slab[o] for o in range(REACH)] + [jnp.zeros_like(block)]
            halves.append(jnp.concatenate(tiles, axis=0))
        rows = lax.dot_general(
            chosen,
            jnp.concatenate(halves, axis=1),
            (((1,), (1,)), ((), ())),
            preferred_element_type=F32,
        )
        for i in range(SLAB):
            dense_sum[i, pl.ds(pl.multiple_of(8 * m, 8), 8), :] = rows[8 * i : 8 * i + 8]
        return 0

    lax.fori_loop(0, RANK // 2, dense_rows, 0, unroll=4)
    for d in TURNS[:3]:
        i = cluster(d)
        dense_send[i] = dense_sum[i].astype(BF16)
        dense_copy(d).start()
    for i in range(SLAB):

        @pl.when(i != c)
        def _():
            set_coefficients(0, i)

    share_order.wait()
    loads[10].wait()

    for a in range(2):
        near_pass(a, 2, False, back_prefix)

        @pl.when(has_above)
        def _():
            for turn in TURNS:
                at, live = last_of(3, SLAB + cluster(turn))
                ahead_send[a, turn] = (back_prefix[at] * live).astype(BF16)
                ahead_copy(a, turn).start()

        def far_back():
            farback_send[a] = lax.dot_general(
                dense[...], coef_own[a], (((0,), (0,)), ((), ())), preferred_element_type=F32
            ).astype(BF16)
            each(rows_above, lambda o: farback_copy(a, o).start())

        if a == 1:
            far_back()

        @pl.when(has_above)
        def _():
            for turn in range(SLAB):
                field_copy(a, turn).wait_recv()

        near_pass(a, 0, True, near_prefix)

        if a == 0:
            for d in TURNS[:3]:
                dense_copy(d).wait_recv()
            total = dense_sum[c]
            for d in range(SLAB - 1):
                total = total + dense_recv[d].astype(F32)
            at = lax.broadcasted_iota(I32, (LANES, LANES), 0)
            wanted = (at & (RANK - 1)) * SLAB + (at >> 5)
            move = jnp.where(lax.broadcasted_iota(I32, (LANES, LANES), 1) == wanted, 1.0, 0.0)
            dense[...] = jnp.dot(
                move.astype(BF16), total.astype(BF16), preferred_element_type=F32
            ).astype(BF16)
            far_back()

        for turn in TURNS:
            i = cluster(turn)

            @pl.when(has_below)
            def _():
                ahead_copy(a, turn).wait_recv()

            at, live = last_of(1, i)
            image = near_prefix[at] * live
            at, live = last_of(3, i)
            image = image + back_prefix[at] * live + ahead_recv[a, turn].astype(F32)
            if turn > 0:
                part_send[a, turn - 1] = image.astype(BF16)
                part_copy(a, turn).start()

        each(rows_above, lambda o: coef_copy(a, o).wait_recv())
        farpart_send[a] = jnp.dot(
            dense[...], coef_ahead[a], preferred_element_type=F32
        ).astype(BF16)
        for d in TURNS[:3]:
            farpart_copy(a, d).start()
        far_total = farpart_send[a, ranks(c), :].astype(F32)

        each(rows_below, lambda o: farback_copy(a, o).wait_recv())
        for o in range(REACH):
            far_total = far_total + farback_recv[a, o].astype(F32)
        for d in TURNS[:3]:
            part_copy(a, d).wait_recv()
            image = image + part_recv[a, d - 1].astype(F32)
        for d in TURNS[:3]:
            farpart_copy(a, d).wait_recv()
            far_total = far_total + farpart_recv[a, d - 1].astype(F32)
        image = image + lax.dot_general(
            far_total.astype(BF16),
            basis_ref[c],
            (((0,), (0,)), ((), ())),
            preferred_element_type=F32,
        )
        images[a][c] = masked(image, sizes_ref[c]).astype(BF16)
        for d in TURNS[:3]:
            image_copy(a, d).start()
        if a == 0:

            @pl.when(has_below)
            def _():
                field_copy(1, 0).start()

            set_coefficients(1, c)
            each(rows_below, lambda o: coef_copy(1, o).start())
        for d in (1, 3, 2):
            image_copy(a, d).wait_recv()
            if a == 0:

                @pl.when(has_below)
                def _():
                    field_copy(1, d).start()

        if a == 0:
            for d in (1, 3, 2):
                set_coefficients(1, cluster(SLAB - d))

    for a in range(2):
        for d in range(1, SLAB):
            part_copy(a, d).wait_send()
            farpart_copy(a, d).wait_send()
            image_copy(a, d).wait_send()
        each(rows_below, lambda o: coef_copy(a, o).wait_send())
        each(rows_above, lambda o: farback_copy(a, o).wait_send())

        @pl.when(has_below)
        def _():
            for turn in range(SLAB):
                field_copy(a, turn).wait_send()

        @pl.when(has_above)
        def _():
            for turn in range(SLAB):
                ahead_copy(a, turn).wait_send()

    for d in range(1, SLAB):
        dense_copy(d).wait_send()


def per_device(n_rows, *arrays):
    arrays = list(arrays)
    arrays[7] = jnp.transpose(arrays[7], (1, 2, 0))
    for n in range(11):
        if arrays[n].size > 1:
            arrays[n] = pltpu.with_memory_space_constraint(arrays[n], pltpu.HBM)
    hbm = pl.BlockSpec(memory_space=pltpu.HBM)
    vmem = pl.BlockSpec(memory_space=pltpu.VMEM)
    image = jax.ShapeDtypeStruct((SLAB, RHS, PANELS), BF16)
    return pl.pallas_call(
        functools.partial(kernel, n_rows),
        out_shape=(image, image),
        in_specs=[hbm] * 11,
        out_specs=(vmem, vmem),
        scratch_shapes=[
            pltpu.VMEM((SLAB, RHS, PANELS), BF16),
            pltpu.VMEM((SLAB, RANK, PANELS), BF16),
            pltpu.SMEM((SLAB,), I32),
            pltpu.VMEM((NEAR, PANELS, PANELS), BF16),
            pltpu.SMEM((NEAR,), I32),
            pltpu.SMEM((NEAR,), I32),
            pltpu.SMEM((1,), I32),
            pltpu.VMEM((RANK, RANK, FAR), BF16),
            pltpu.VMEM((FAR,), I32),
            pltpu.VMEM((FAR,), I32),
            pltpu.SMEM((1,), I32),
            pltpu.VMEM((SLAB, RHS, PANELS), BF16),
            pltpu.VMEM((SLAB, RHS, PANELS), BF16),
            pltpu.VMEM((SLAB, RHS, PANELS), BF16),
            pltpu.VMEM((8, LANES), I32),
            pltpu.SMEM((8, LANES), I32),
            pltpu.VMEM((2, SLAB * RANK, RHS), BF16),
            pltpu.VMEM((2, (REACH + 1) * RANK, RHS), BF16),
            pltpu.VMEM((SLAB, SLAB * RANK, 2 * LANES), F32),
            pltpu.VMEM((SLAB, SLAB * RANK, 2 * LANES), BF16),
            pltpu.VMEM((SLAB - 1, SLAB * RANK, 2 * LANES), BF16),
            pltpu.VMEM((SLAB * RANK, 2 * LANES), BF16),
            pltpu.VMEM((NEAR, RHS, PANELS), F32),
            pltpu.VMEM((NEAR, RHS, PANELS), F32),
            pltpu.VMEM((2, SLAB, RHS, PANELS), BF16),
            pltpu.VMEM((2, SLAB, RHS, PANELS), BF16),
            pltpu.VMEM((2, SLAB - 1, RHS, PANELS), BF16),
            pltpu.VMEM((2, SLAB - 1, RHS, PANELS), BF16),
            pltpu.VMEM((2, SLAB * RANK, RHS), BF16),
            pltpu.VMEM((2, SLAB - 1, RANK, RHS), BF16),
            pltpu.VMEM((2, (REACH + 1) * RANK, RHS), BF16),
            pltpu.VMEM((2, REACH, RANK, RHS), BF16),
            pltpu.SemaphoreType.DMA((N_SEMS,)),
            pltpu.SemaphoreType.DMA((N_SEMS,)),
            pltpu.SemaphoreType.DMA((12,)),
        ],
        compiler_params=pltpu.CompilerParams(
            collective_id=0, has_side_effects=True, vmem_limit_bytes=40 * 1024 * 1024
        ),
    )(*arrays)


def solution(mesh):
    placed = (
        P("row", None, None),
        P("row", None, None),
        P("row"),
        P(("row", "col"), None, None),
        P(("row", "col")),
        P(("row", "col")),
        P(("row", "col")),
        P(("row", "col"), None, None),
        P(("row", "col")),
        P(("row", "col")),
        P(("row", "col")),
    )
    return jax.shard_map(
        functools.partial(per_device, mesh.shape["row"]),
        mesh=mesh,
        in_specs=placed,
        out_specs=(P("row", None, None), P("row", None, None)),
        check_vma=False,
    )
```

time: 74.1 us -> 48.5 us (0.65)
  the two profiles are of different devices: /device:TPU:2 before, /device:TPU:512 now
where the time goes in v2:
time: 48.5 us; the launch traced here: 48.4 us
  Pallas kernels  45 us (93%)
  between operations  1.93 us (4%)
  local copies, waits for them, and re-layouts  1.41 us (3%)
    pallas_call x1, Pallas kernels, per_device(): pl.pallas_call(functools.partial(kernel, n_rows), out_shape=(image, image...  45 us
    unnamed x2, local copies, waits for them, and re-layouts  1.41 us

profile of v2, /device:TPU:512, one launch (start us, length us, event | category | flops | bytes accessed | tf_op | source)
XLA Modules:
  0.0 48.4 jit_solution(10354627115114359099)
XLA Ops:
  1.9 45.0 %shard_map.122 = (bf16[4,128,256]{2,1,0:T(8,128)(2,1)S(1)}, bf16[4,128,256]{2,1,0:T(8,128)(2,1)S(1)}) custom-call(bf16[4,128,256]{2,1,0:T(8,128)(2,1)} %charges_hbm.1, bf16[4,32,256]{2,1,0:T(8,128)(2,1)} %basis_hbm.1, s32[4]{0:T(128)} %sizes_hbm.1, bf16[16,256,256]{2,1,0:T(8,128)(2,1)} %blocks_hbm.1, s32[16]{0:T(128)} %near_rows_hbm.1, s32[16]{0:T(128)} %near_cols_hbm.1, ...), custom_call_target="tpu_custom_call" | custom-call | tf_op jit(solution)/shard_map/pallas_call | solution.py:481
  47.0 0.7 %copy.17 = bf16[4,128,256]{2,1,0:T(8,128)(2,1)} copy(bf16[4,128,256]{2,1,0:T(8,128)(2,1)S(1)} %get-tuple-element.4) | data formatting | bytes 524288
  47.7 0.7 %copy.18 = bf16[4,128,256]{2,1,0:T(8,128)(2,1)} copy(bf16[4,128,256]{2,1,0:T(8,128)(2,1)S(1)} %get-tuple-element.5) | data formatting | bytes 524288

commit v3 on v2

v3 whole, which is shorter than its diff:
```python
import functools

import jax
import jax.numpy as jnp
from jax import lax
from jax.experimental import pallas as pl
from jax.experimental.pallas import tpu as pltpu
from jax.sharding import PartitionSpec as P

MESH = pl.DeviceIdType.MESH
F32 = jnp.float32
BF16 = jnp.bfloat16
I32 = jnp.int32

SLAB = 4
REACH = 7
TILES = 4
NEAR = 16
FAR = 128
RANK = 32
RHS = 128
PANELS = 256
LANES = 128
HALF = RHS // 2
UNROLL = 8

FIELD, AHEAD, PART, IMAGE, COEF, FARBACK, FARPART, SIBLING, PER_APPLY = 0, 8, 16, 22, 28, 32, 36, 43, 44
DENSE = 2 * PER_APPLY
N_SEMS = DENSE + 7
TURNS = (2, 1, 3, 0)


def sort_keys(unique_keys):
    across = jnp.broadcast_to(unique_keys, (LANES, LANES))
    down = across.T
    rank = jnp.sum(jnp.where(across < down, 1, 0).astype(I32), axis=1, keepdims=True)
    lane = lax.broadcasted_iota(I32, (LANES, LANES), 1)
    ordered = jnp.sum(jnp.where(rank == lane, down, 0), axis=0, keepdims=True)
    return ordered, down


def count_upto(down, shift):
    lane = lax.broadcasted_iota(I32, (LANES, LANES), 1)
    return jnp.sum(jnp.where((down >> shift) <= lane, 1, 0).astype(I32), axis=0, keepdims=True)


def kernel(
    n_rows,
    charges_hbm,
    basis_hbm,
    sizes_hbm,
    blocks_hbm,
    near_rows_hbm,
    near_cols_hbm,
    near_live_hbm,
    couplings_hbm,
    far_rows_hbm,
    far_cols_hbm,
    far_live_hbm,
    first_image,
    second_image,
    charges,
    basis_ref,
    sizes_ref,
    blocks,
    near_rows_ref,
    near_cols_ref,
    near_live_ref,
    couplings,
    far_rows_ref,
    far_cols_ref,
    far_live_ref,
    masked_low,
    masked_high,
    own_low,
    own_high,
    next_first_low,
    next_first_high,
    next_second_low,
    next_second_high,
    order_v,
    order_s,
    coef_own,
    coef_sibling,
    coef_ahead,
    dense_sum,
    dense_send,
    dense_recv,
    dense,
    near_prefix,
    back_prefix,
    ahead_send,
    ahead_recv,
    part_send,
    part_recv,
    farpart_send,
    farpart_recv,
    farback_send,
    farback_recv,
    send_sem,
    recv_sem,
    load_sem,
):
    r = lax.axis_index("row")
    c = lax.axis_index("col")
    own = ((masked_low, masked_high), (own_low, own_high))
    ahead = ((next_first_low, next_first_high), (next_second_low, next_second_high))
    halves = (slice(0, HALF), slice(HALF, RHS))
    odd = lax.rem(r, 2)
    sibling = r + 1 - 2 * odd
    rows_above = jnp.minimum(TILES - odd, (n_rows - 1 - r) // 2)
    rows_below = jnp.minimum(TILES - odd, r // 2)
    has_above = r < n_rows - 1
    has_below = r > 0

    def up(o):
        return (lax.rem(r + o, n_rows), c)

    def down(o):
        return (lax.rem(r + n_rows - o, n_rows), c)

    def beside(d):
        return (r, lax.rem(c + d, SLAB))

    def across(d):
        return (sibling, lax.rem(c + d, SLAB))

    def cluster(turn):
        return lax.rem(c + turn, SLAB)

    def ranks(i):
        return pl.ds(pl.multiple_of(i * RANK, RANK), RANK)

    def remote(src, dst, at, device):
        return pltpu.make_async_remote_copy(
            src_ref=src,
            dst_ref=dst,
            send_sem=send_sem.at[at],
            recv_sem=recv_sem.at[at],
            device_id=device,
            device_id_type=MESH,
        )

    def field_copy(a, turn, h):
        i = cluster(SLAB - turn)
        at = a * PER_APPLY + FIELD + SLAB * h + turn
        return remote(own[a][h].at[i], ahead[a][h].at[i], at, down(1))

    def coef_copy(a, m):
        return remote(
            coef_own.at[a, ranks(c), :],
            coef_ahead.at[a, ranks(m - 1 + odd), :],
            a * PER_APPLY + COEF + m - 1,
            down(2 * m),
        )

    def sibling_copy(a):
        return remote(
            coef_own.at[a], coef_sibling.at[a], a * PER_APPLY + SIBLING, across(0)
        )

    def ahead_copy(a, turn, h):
        return remote(
            ahead_send.at[a, turn, halves[h], :],
            ahead_recv.at[a, turn, halves[h], :],
            a * PER_APPLY + AHEAD + SLAB * h + turn,
            up(1),
        )

    def part_copy(a, d, h):
        return remote(
            part_send.at[a, d - 1, halves[h], :],
            part_recv.at[a, d - 1, halves[h], :],
            a * PER_APPLY + PART + (SLAB - 1) * h + d - 1,
            beside(d),
        )

    def farpart_copy(a, d):
        return remote(
            farpart_send.at[a, ranks(cluster(d)), :],
            farpart_recv.at[a, d - 1],
            a * PER_APPLY + FARPART + d - 1,
            beside(d),
        )

    def farcross_copy(a, d):
        return remote(
            farpart_send.at[a, ranks(SLAB + cluster(d)), :],
            farpart_recv.at[a, SLAB - 1 + d],
            a * PER_APPLY + FARPART + SLAB - 1 + d,
            across(d),
        )

    def farback_copy(a, m):
        return remote(
            farback_send.at[a, ranks(m - 1 + odd), :],
            farback_recv.at[a, m - 1],
            a * PER_APPLY + FARBACK + m - 1,
            up(2 * m),
        )

    def image_copy(a, d, h):
        mine = own[1][h].at[c] if a == 0 else second_image.at[c, halves[h], :]
        return remote(mine, mine, a * PER_APPLY + IMAGE + (SLAB - 1) * h + d - 1, beside(d))

    def dense_copy(d):
        return remote(
            dense_send.at[1, cluster(d)], dense_recv.at[d - 1], DENSE + d - 1, beside(d)
        )

    def dense_cross_copy(d):
        return remote(
            dense_send.at[0, cluster(d)],
            dense_recv.at[SLAB - 1 + d],
            DENSE + SLAB - 1 + d,
            across(d),
        )

    def each(count, act):
        def step(o, _):
            act(o)
            return 0

        lax.fori_loop(1, count + 1, step, 0)

    loads = [
        pltpu.make_async_copy(source, target, load_sem.at[at])
        for at, (source, target) in enumerate(
            (
                (charges_hbm, charges),
                (sizes_hbm, sizes_ref),
                (basis_hbm, basis_ref),
                (near_rows_hbm, near_rows_ref),
                (near_cols_hbm, near_cols_ref),
                (near_live_hbm, near_live_ref),
                (far_rows_hbm, far_rows_ref),
                (far_cols_hbm, far_cols_ref),
                (far_live_hbm, far_live_ref),
                (couplings_hbm, couplings),
                (blocks_hbm, blocks),
            )
        )
    ]
    for load in loads:
        load.start()

    coef_ahead[...] = jnp.zeros_like(coef_ahead)
    farback_recv[...] = jnp.zeros_like(farback_recv)

    @pl.when(jnp.logical_not(has_above))
    def _():
        for a in range(2):
            for h in range(2):
                ahead[a][h][...] = jnp.zeros_like(ahead[a][h])

    @pl.when(jnp.logical_not(has_below))
    def _():
        ahead_recv[...] = jnp.zeros_like(ahead_recv)

    barrier = pltpu.get_barrier_semaphore()

    def greet(device):
        pl.semaphore_signal(barrier, inc=1, device_id=device, device_id_type=MESH)

    for d in range(1, SLAB):
        greet(beside(d))
    for d in range(SLAB):
        greet(across(d))
    each(rows_above, lambda m: greet(up(2 * m)))
    each(rows_below, lambda m: greet(down(2 * m)))
    has_outer = jnp.where(odd == 1, r < n_rows - 1, r > 0)

    @pl.when(has_outer)
    def _():
        greet(up(jnp.where(odd == 1, 1, n_rows - 1)))


    def masked(values, size):
        panel = lax.broadcasted_iota(I32, values.shape, 1)
        return jnp.where(panel < size, values, jnp.zeros_like(values))

    def last_of(row, group):
        upto = order_s[row, group]
        before = jnp.where(group > 0, order_s[row, jnp.maximum(group - 1, 0)], 0)
        return jnp.maximum(upto - 1, 0), (upto > before).astype(F32)

    def set_coefficients(a, i):
        coef_own[a, ranks(i), :] = lax.dot_general(
            basis_ref[i],
            jnp.concatenate([own[a][0][i], own[a][1][i]], axis=0),
            (((1,), (1,)), ((), ())),
            preferred_element_type=F32,
        ).astype(BF16)

    def near_pass(a, order_row, forward, prefix, h):
        def slot(k, carry):
            total, previous = carry
            key = order_s[order_row, k]
            group = key >> 7
            other = (key >> 4) & 7
            source = own[a][h][other & 3]
            if forward:
                source = jnp.where(other < SLAB, source, ahead[a][h][other & 3])
            block = blocks[key & 15]
            product = lax.dot_general(
                source,
                block,
                (((1,), (1 if forward else 0,)), ((), ())),
                preferred_element_type=F32,
            )
            total = total * (group == previous).astype(F32) + product
            prefix[h, k] = total
            return total, group

        start = (jnp.zeros((HALF, PANELS), F32), jnp.int32(-1))
        lax.fori_loop(0, NEAR, slot, start, unroll=UNROLL)

    for load in loads[0:3]:
        load.wait()
    for i in range(SLAB):
        values = masked(charges[i], sizes_ref[i])
        for h in range(2):
            own[0][h][i] = values[halves[h]]
    set_coefficients(0, c)

    first = r * SLAB
    lane = lax.broadcasted_iota(I32, (1, LANES), 1)
    for load in loads[3:6]:
        load.wait()
    near_used = near_live_ref[0]
    by_row = jnp.broadcast_to((1 << 16) + lane, (1, LANES))
    by_col = by_row
    for s in range(NEAR):
        row = jnp.clip(near_rows_ref[s] - first, 0, SLAB - 1)
        col = jnp.clip(near_cols_ref[s] - first, 0, 2 * SLAB - 1)
        used = s < near_used
        row_key = (jnp.where(used, row, SLAB) << 7) + (col << 4) + s
        col_key = (jnp.where(used, col, 2 * SLAB) << 7) + (row << 4) + s
        by_row = jnp.where(lane == s, row_key, by_row)
        by_col = jnp.where(lane == s, col_key, by_col)
    for at, keys in enumerate((by_row, by_col)):
        ordered, laid = sort_keys(keys)
        order_v[2 * at : 2 * at + 1, :] = ordered
        order_v[2 * at + 1 : 2 * at + 2, :] = count_upto(laid, 7)
    order_v[4:8, :] = jnp.zeros((4, LANES), I32)
    share_order = pltpu.make_async_copy(order_v, order_s, load_sem.at[11])
    share_order.start()

    for load in loads[6:9]:
        load.wait()
    far_row = jnp.clip(far_rows_ref[...] - first, 0, SLAB - 1).reshape(1, LANES)
    far_col = jnp.clip(far_cols_ref[...] - first - SLAB, 0, REACH * SLAB - 1).reshape(1, LANES)
    far_slab = far_col >> 2
    far_tile = (far_slab >> 1) + jnp.where((far_slab & 1) == 1, TILES + odd, 0)
    far_key = (far_col & 3) * (2 * SLAB) + far_row
    far_key = jnp.where(lane < far_live_ref[0], far_key, -2 * SLAB)
    loads[9].wait()
    target = lax.broadcasted_iota(I32, (8 * SLAB, 2 * LANES), 0)
    chosen = jnp.where(target == jnp.concatenate([far_key, far_key + SLAB], axis=1), 1.0, 0.0)
    chosen = chosen.astype(BF16)
    in_slab = [
        jnp.broadcast_to(jnp.where(far_tile == o, 1.0, 0.0), (RANK, LANES)).astype(BF16)
        for o in range(2 * TILES)
    ]

    def dense_rows(m, _):
        halves = []
        for half in range(2):
            block = couplings[2 * m + half]
            tiles = [block * in_slab[o] for o in range(2 * TILES)]
            halves.append(jnp.concatenate(tiles, axis=0))
        rows = lax.dot_general(
            chosen,
            jnp.concatenate(halves, axis=1),
            (((1,), (1,)), ((), ())),
            preferred_element_type=F32,
        )
        for i in range(SLAB):
            dense_sum[i, pl.ds(pl.multiple_of(8 * m, 8), 8), :] = rows[8 * i : 8 * i + 8]
        return 0

    lax.fori_loop(0, RANK // 2, dense_rows, 0, unroll=4)
    pl.semaphore_wait(
        barrier, 2 * SLAB - 1 + rows_above + rows_below + jnp.where(has_outer, 1, 0)
    )

    @pl.when(has_below)
    def _():
        for h in range(2):
            for turn in range(SLAB):
                field_copy(0, turn, h).start()

    for d in TURNS:
        i = cluster(d)
        dense_send[0, i] = dense_sum[i][:, :LANES].astype(BF16)
        dense_cross_copy(d).start()
        if d > 0:
            dense_send[1, i] = dense_sum[i][:, LANES:].astype(BF16)
            dense_copy(d).start()
    each(rows_below, lambda m: coef_copy(0, m).start())

    for i in range(SLAB):

        @pl.when(i != c)
        def _():
            set_coefficients(0, i)

    sibling_copy(0).start()

    def own_tile(a):
        @pl.when(odd == 1)
        def _():
            coef_ahead[a, 0:RANK, :] = coef_own[a, ranks(c), :]

    own_tile(0)
    share_order.wait()
    loads[10].wait()

    for a in range(2):
        for h in range(2):
            if a == 1:
                for d in (1, 3, 2):
                    image_copy(0, d, h).wait_recv()

                    @pl.when(has_below)
                    def _():
                        field_copy(1, d, h).start()

            near_pass(a, 2, False, back_prefix, h)

            @pl.when(has_above)
            def _():
                for turn in TURNS:
                    at, live = last_of(3, SLAB + cluster(turn))
                    ahead_send[a, turn, halves[h], :] = (back_prefix[h, at] * live).astype(BF16)
                    ahead_copy(a, turn, h).start()

        def far_back():
            sibling_copy(a).wait_recv()
            both = jnp.concatenate([coef_own[a], coef_sibling[a]], axis=0)
            farback_send[a] = lax.dot_general(
                dense[...], both, (((0,), (0,)), ((), ())), preferred_element_type=F32
            ).astype(BF16)
            each(rows_above, lambda m: farback_copy(a, m).start())

        if a == 1:
            for d in (1, 3, 2):
                set_coefficients(1, cluster(SLAB - d))
            sibling_copy(1).start()

        own_parts = []
        for h in range(2):
            @pl.when(has_above)
            def _():
                for turn in range(SLAB):
                    field_copy(a, turn, h).wait_recv()

            near_pass(a, 0, True, near_prefix, h)

            for turn in TURNS:
                i = cluster(turn)

                @pl.when(has_below)
                def _():
                    ahead_copy(a, turn, h).wait_recv()

                at, live = last_of(1, i)
                image = near_prefix[h, at] * live
                at, live = last_of(3, i)
                image = image + back_prefix[h, at] * live
                image = image + ahead_recv[a, turn, halves[h], :].astype(F32)
                if turn > 0:
                    part_send[a, turn - 1, halves[h], :] = image.astype(BF16)
                    part_copy(a, turn, h).start()
            own_parts.append(image)

            if h == 0:
                if a == 0:
                    for d in TURNS:
                        dense_cross_copy(d).wait_recv()
                        if d > 0:
                            dense_copy(d).wait_recv()
                    at = lax.broadcasted_iota(I32, (LANES, LANES), 0)
                    wanted = (at & (RANK - 1)) * SLAB + (at >> 5)
                    move = jnp.where(lax.broadcasted_iota(I32, (LANES, LANES), 1) == wanted, 1.0, 0.0)
                    move = move.astype(BF16)
                    total = dense_sum[c][:, LANES:]
                    for d in range(SLAB - 1):
                        total = total + dense_recv[d].astype(F32)
                    dense[0:LANES, :] = jnp.dot(
                        move, total.astype(BF16), preferred_element_type=F32
                    ).astype(BF16)
                    total = dense_recv[SLAB - 1].astype(F32)
                    for d in range(1, SLAB):
                        total = total + dense_recv[SLAB - 1 + d].astype(F32)
                    dense[LANES:, :] = jnp.dot(
                        move, total.astype(BF16), preferred_element_type=F32
                    ).astype(BF16)
                far_back()

                each(rows_above, lambda m: coef_copy(a, m).wait_recv())
                farpart_send[a] = jnp.dot(
                    dense[...], coef_ahead[a], preferred_element_type=F32
                ).astype(BF16)
                for d in TURNS:
                    farcross_copy(a, d).start()
                    if d > 0:
                        farpart_copy(a, d).start()
        far_total = farpart_send[a, ranks(c), :].astype(F32)
        far_total = far_total + jnp.where(odd == 1, farback_send[a, 0:RANK, :], 0).astype(F32)

        each(rows_below, lambda m: farback_copy(a, m).wait_recv())
        for m in range(TILES):
            far_total = far_total + farback_recv[a, m].astype(F32)
        for d in TURNS:
            farcross_copy(a, d).wait_recv()
            if d > 0:
                farpart_copy(a, d).wait_recv()
        for d in range(2 * SLAB - 1):
            far_total = far_total + farpart_recv[a, d].astype(F32)
        far_image = lax.dot_general(
            far_total.astype(BF16),
            basis_ref[c],
            (((0,), (0,)), ((), ())),
            preferred_element_type=F32,
        )
        for h in range(2):
            image = own_parts[h] + far_image[halves[h]]
            for d in TURNS[:3]:
                part_copy(a, d, h).wait_recv()
                image = image + part_recv[a, d - 1, halves[h], :].astype(F32)
            image = masked(image, sizes_ref[c]).astype(BF16)
            if a == 0:
                own[1][h][c] = image
            else:
                second_image[c, halves[h], :] = image
            for d in TURNS[:3]:
                image_copy(a, d, h).start()
            if a == 0:

                @pl.when(has_below)
                def _():
                    field_copy(1, 0, h).start()

        if a == 0:
            set_coefficients(1, c)
            each(rows_below, lambda m: coef_copy(1, m).start())
            own_tile(1)

    for h in range(2):
        first_image[:, halves[h], :] = own[1][h][...]
        for d in (1, 3, 2):
            image_copy(1, d, h).wait_recv()

    for a in range(2):
        for d in range(1, SLAB):
            farpart_copy(a, d).wait_send()
            for h in range(2):
                part_copy(a, d, h).wait_send()
                image_copy(a, d, h).wait_send()
        for d in range(SLAB):
            farcross_copy(a, d).wait_send()
        sibling_copy(a).wait_send()
        each(rows_below, lambda m: coef_copy(a, m).wait_send())
        each(rows_above, lambda m: farback_copy(a, m).wait_send())

        @pl.when(has_below)
        def _():
            for turn in range(SLAB):
                for h in range(2):
                    field_copy(a, turn, h).wait_send()

        @pl.when(has_above)
        def _():
            for turn in range(SLAB):
                for h in range(2):
                    ahead_copy(a, turn, h).wait_send()

    for d in range(1, SLAB):
        dense_copy(d).wait_send()
    for d in range(SLAB):
        dense_cross_copy(d).wait_send()


def per_device(n_rows, *arrays):
    arrays = list(arrays)
    arrays[7] = jnp.transpose(arrays[7], (1, 2, 0))
    for n in range(11):
        if arrays[n].size > 1:
            arrays[n] = pltpu.with_memory_space_constraint(arrays[n], pltpu.HBM)
    hbm = pl.BlockSpec(memory_space=pltpu.HBM)
    vmem = pl.BlockSpec(memory_space=pltpu.VMEM)
    image = jax.ShapeDtypeStruct((SLAB, RHS, PANELS), BF16)
    return pl.pallas_call(
        functools.partial(kernel, n_rows),
        out_shape=(image, image),
        in_specs=[hbm] * 11,
        out_specs=(vmem, vmem),
        scratch_shapes=[
            pltpu.VMEM((SLAB, RHS, PANELS), BF16),
            pltpu.VMEM((SLAB, RANK, PANELS), BF16),
            pltpu.SMEM((SLAB,), I32),
            pltpu.VMEM((NEAR, PANELS, PANELS), BF16),
            pltpu.SMEM((NEAR,), I32),
            pltpu.SMEM((NEAR,), I32),
            pltpu.SMEM((1,), I32),
            pltpu.VMEM((RANK, RANK, FAR), BF16),
            pltpu.VMEM((FAR,), I32),
            pltpu.VMEM((FAR,), I32),
            pltpu.SMEM((1,), I32),
            pltpu.VMEM((SLAB, HALF, PANELS), BF16),
            pltpu.VMEM((SLAB, HALF, PANELS), BF16),
            pltpu.VMEM((SLAB, HALF, PANELS), BF16),
            pltpu.VMEM((SLAB, HALF, PANELS), BF16),
            pltpu.VMEM((SLAB, HALF, PANELS), BF16),
            pltpu.VMEM((SLAB, HALF, PANELS), BF16),
            pltpu.VMEM((SLAB, HALF, PANELS), BF16),
            pltpu.VMEM((SLAB, HALF, PANELS), BF16),
            pltpu.VMEM((8, LANES), I32),
            pltpu.SMEM((8, LANES), I32),
            pltpu.VMEM((2, SLAB * RANK, RHS), BF16),
            pltpu.VMEM((2, SLAB * RANK, RHS), BF16),
            pltpu.VMEM((2, TILES * RANK, RHS), BF16),
            pltpu.VMEM((SLAB, SLAB * RANK, 2 * LANES), F32),
            pltpu.VMEM((2, SLAB, SLAB * RANK, LANES), BF16),
            pltpu.VMEM((2 * SLAB - 1, SLAB * RANK, LANES), BF16),
            pltpu.VMEM((2 * SLAB * RANK, LANES), BF16),
            pltpu.VMEM((2, NEAR, HALF, PANELS), F32),
            pltpu.VMEM((2, NEAR, HALF, PANELS), F32),
            pltpu.VMEM((2, SLAB, RHS, PANELS), BF16),
            pltpu.VMEM((2, SLAB, RHS, PANELS), BF16),
            pltpu.VMEM((2, SLAB - 1, RHS, PANELS), BF16),
            pltpu.VMEM((2, SLAB - 1, RHS, PANELS), BF16),
            pltpu.VMEM((2, 2 * SLAB * RANK, RHS), BF16),
            pltpu.VMEM((2, 2 * SLAB - 1, RANK, RHS), BF16),
            pltpu.VMEM((2, TILES * RANK, RHS), BF16),
            pltpu.VMEM((2, TILES, RANK, RHS), BF16),
            pltpu.SemaphoreType.DMA((N_SEMS,)),
            pltpu.SemaphoreType.DMA((N_SEMS,)),
            pltpu.SemaphoreType.DMA((12,)),
        ],
        compiler_params=pltpu.CompilerParams(
            collective_id=0, has_side_effects=True, vmem_limit_bytes=40 * 1024 * 1024
        ),
    )(*arrays)


def solution(mesh):
    placed = (
        P("row", None, None),
        P("row", None, None),
        P("row"),
        P(("row", "col"), None, None),
        P(("row", "col")),
        P(("row", "col")),
        P(("row", "col")),
        P(("row", "col"), None, None),
        P(("row", "col")),
        P(("row", "col")),
        P(("row", "col")),
    )
    return jax.shard_map(
        functools.partial(per_device, mesh.shape["row"]),
        mesh=mesh,
        in_specs=placed,
        out_specs=(P("row", None, None), P("row", None, None)),
        check_vma=False,
    )
```

time: 48.5 us -> 47.3 us (0.975)
  the two profiles are of different devices: /device:TPU:512 before, /device:TPU:1 now
where the time goes in v3:
time: 47.3 us; the launch traced here: 47.1 us
  Pallas kernels  43.7 us (92%)
  between operations  1.93 us (4%)
  local copies, waits for them, and re-layouts  1.41 us (3%)
    pallas_call x1, Pallas kernels, per_device(): pl.pallas_call(functools.partial(kernel, n_rows), out_shape=(image, image...  43.7 us
    unnamed x2, local copies, waits for them, and re-layouts  1.41 us

profile of v3, /device:TPU:1, one launch (start us, length us, event | category | flops | bytes accessed | tf_op | source)
XLA Modules:
  0.0 47.1 jit_solution(17241686834847972304)
XLA Ops:
  1.9 43.7 %shard_map.122 = (bf16[4,128,256]{2,1,0:T(8,128)(2,1)S(1)}, bf16[4,128,256]{2,1,0:T(8,128)(2,1)S(1)}) custom-call(bf16[4,128,256]{2,1,0:T(8,128)(2,1)} %charges_hbm.1, bf16[4,32,256]{2,1,0:T(8,128)(2,1)} %basis_hbm.1, s32[4]{0:T(128)} %sizes_hbm.1, bf16[16,256,256]{2,1,0:T(8,128)(2,1)} %blocks_hbm.1, s32[16]{0:T(128)} %near_rows_hbm.1, s32[16]{0:T(128)} %near_cols_hbm.1, ...), custom_call_target="tpu_custom_call" | custom-call | tf_op jit(solution)/shard_map/pallas_call | solution.py:594
  45.7 0.7 %copy.17 = bf16[4,128,256]{2,1,0:T(8,128)(2,1)} copy(bf16[4,128,256]{2,1,0:T(8,128)(2,1)S(1)} %get-tuple-element.4) | data formatting | bytes 524288
  46.4 0.7 %copy.18 = bf16[4,128,256]{2,1,0:T(8,128)(2,1)} copy(bf16[4,128,256]{2,1,0:T(8,128)(2,1)S(1)} %get-tuple-element.5) | data formatting | bytes 524288

commit v4 on v3

--- a/solution.py
+++ b/solution.py
@@ -23,8 +23,9 @@
 LANES = 128
 HALF = RHS // 2
 UNROLL = 8
-
-FIELD, AHEAD, PART, IMAGE, COEF, FARBACK, FARPART, SIBLING, PER_APPLY = 0, 8, 16, 22, 28, 32, 36, 43, 44
+BACK_AT, PART_AT = (1, -1), (1, 0)
+
+FIELD, AHEAD, PART, IMAGE, COEF, FARBACK, FARPART, SHARE, PER_APPLY = 0, 8, 16, 22, 28, 32, 36, 43, 50
 DENSE = 2 * PER_APPLY
 N_SEMS = DENSE + 7
 TURNS = (2, 1, 3, 0)
@@ -154,9 +155,19 @@
             down(2 * m),
         )
 
-    def sibling_copy(a):
-        return remote(
-            coef_own.at[a], coef_sibling.at[a], a * PER_APPLY + SIBLING, across(0)
+    def sibling_copy():
+        return remote(coef_own.at[0], coef_sibling.at[0], SHARE, across(0))
+
+    def share_copy(d):
+        mine = coef_own.at[1, ranks(c), :]
+        return remote(mine, mine, PER_APPLY + SHARE + d - 1, beside(d))
+
+    def share_cross_copy(d):
+        return remote(
+            coef_own.at[1, ranks(c), :],
+            coef_sibling.at[1, ranks(c), :],
+            PER_APPLY + SHARE + SLAB - 1 + d,
+            across(d),
         )
 
     def ahead_copy(a, turn, h):
@@ -384,12 +395,6 @@
         barrier, 2 * SLAB - 1 + rows_above + rows_below + jnp.where(has_outer, 1, 0)
     )
 
-    @pl.when(has_below)
-    def _():
-        for h in range(2):
-            for turn in range(SLAB):
-                field_copy(0, turn, h).start()
-
     for d in TURNS:
         i = cluster(d)
         dense_send[0, i] = dense_sum[i][:, :LANES].astype(BF16)
@@ -399,13 +404,19 @@
             dense_copy(d).start()
     each(rows_below, lambda m: coef_copy(0, m).start())
 
+    @pl.when(has_below)
+    def _():
+        for h in range(2):
+            for turn in range(SLAB):
+                field_copy(0, turn, h).start()
+
     for i in range(SLAB):
 
         @pl.when(i != c)
         def _():
             set_coefficients(0, i)
 
-    sibling_copy(0).start()
+    sibling_copy().start()
 
     def own_tile(a):
         @pl.when(odd == 1)
@@ -415,6 +426,56 @@
     own_tile(0)
     share_order.wait()
     loads[10].wait()
+
+    def far_back(a):
+        if a == 0:
+            for d in TURNS:
+                dense_cross_copy(d).wait_recv()
+                if d > 0:
+                    dense_copy(d).wait_recv()
+            at = lax.broadcasted_iota(I32, (LANES, LANES), 0)
+            wanted = (at & (RANK - 1)) * SLAB + (at >> 5)
+            move = jnp.where(lax.broadcasted_iota(I32, (LANES, LANES), 1) == wanted, 1.0, 0.0)
+            move = move.astype(BF16)
+            total = dense_sum[c][:, LANES:]
+            for d in range(SLAB - 1):
+                total = total + dense_recv[d].astype(F32)
+            dense[0:LANES, :] = jnp.dot(
+                move, total.astype(BF16), preferred_element_type=F32
+            ).astype(BF16)
+            total = dense_recv[SLAB - 1].astype(F32)
+            for d in range(1, SLAB):
+                total = total + dense_recv[SLAB - 1 + d].astype(F32)
+            dense[LANES:, :] = jnp.dot(
+                move, total.astype(BF16), preferred_element_type=F32
+            ).astype(BF16)
+            sibling_copy().wait_recv()
+        else:
+            for d in TURNS:
+                share_cross_copy(d).wait_recv()
+                if d > 0:
+                    share_copy(d).wait_recv()
+        both = jnp.concatenate([coef_own[a], coef_sibling[a]], axis=0)
+        farback_send[a] = lax.dot_general(
+            dense[...], both, (((0,), (0,)), ((), ())), preferred_element_type=F32
+        ).astype(BF16)
+        each(rows_above, lambda m: farback_copy(a, m).start())
+
+    def far_part(a):
+        each(rows_above, lambda m: coef_copy(a, m).wait_recv())
+        farpart_send[a] = jnp.dot(
+            dense[...], coef_ahead[a], preferred_element_type=F32
+        ).astype(BF16)
+        for d in TURNS:
+            farcross_copy(a, d).start()
+            if d > 0:
+                farpart_copy(a, d).start()
+
+    def stage(a, at):
+        if at == BACK_AT[a]:
+            far_back(a)
+        if at == PART_AT[a]:
+            far_part(a)
 
     for a in range(2):
         for h in range(2):
@@ -435,18 +496,7 @@
                     ahead_send[a, turn, halves[h], :] = (back_prefix[h, at] * live).astype(BF16)
                     ahead_copy(a, turn, h).start()
 
-        def far_back():
-            sibling_copy(a).wait_recv()
-            both = jnp.concatenate([coef_own[a], coef_sibling[a]], axis=0)
-            farback_send[a] = lax.dot_general(
-                dense[...], both, (((0,), (0,)), ((), ())), preferred_element_type=F32
-            ).astype(BF16)
-            each(rows_above, lambda m: farback_copy(a, m).start())
-
-        if a == 1:
-            for d in (1, 3, 2):
-                set_coefficients(1, cluster(SLAB - d))
-            sibling_copy(1).start()
+            stage(a, h - 1)
 
         own_parts = []
         for h in range(2):
@@ -474,38 +524,8 @@
                     part_copy(a, turn, h).start()
             own_parts.append(image)
 
-            if h == 0:
-                if a == 0:
-                    for d in TURNS:
-                        dense_cross_copy(d).wait_recv()
-                        if d > 0:
-                            dense_copy(d).wait_recv()
-                    at = lax.broadcasted_iota(I32, (LANES, LANES), 0)
-                    wanted = (at & (RANK - 1)) * SLAB + (at >> 5)
-                    move = jnp.where(lax.broadcasted_iota(I32, (LANES, LANES), 1) == wanted, 1.0, 0.0)
-                    move = move.astype(BF16)
-                    total = dense_sum[c][:, LANES:]
-                    for d in range(SLAB - 1):
-                        total = total + dense_recv[d].astype(F32)
-                    dense[0:LANES, :] = jnp.dot(
-                        move, total.astype(BF16), preferred_element_type=F32
-                    ).astype(BF16)
-                    total = dense_recv[SLAB - 1].astype(F32)
-                    for d in range(1, SLAB):
-                        total = total + dense_recv[SLAB - 1 + d].astype(F32)
-                    dense[LANES:, :] = jnp.dot(
-                        move, total.astype(BF16), preferred_element_type=F32
-                    ).astype(BF16)
-                far_back()
-
-                each(rows_above, lambda m: coef_copy(a, m).wait_recv())
-                farpart_send[a] = jnp.dot(
-                    dense[...], coef_ahead[a], preferred_element_type=F32
-                ).astype(BF16)
-                for d in TURNS:
-                    farcross_copy(a, d).start()
-                    if d > 0:
-                        farpart_copy(a, d).start()
+            stage(a, 1 + h)
+
         far_total = farpart_send[a, ranks(c), :].astype(F32)
         far_total = far_total + jnp.where(odd == 1, farback_send[a, 0:RANK, :], 0).astype(F32)
 
@@ -544,6 +564,10 @@
 
         if a == 0:
             set_coefficients(1, c)
+            for d in TURNS:
+                share_cross_copy(d).start()
+                if d > 0:
+                    share_copy(d).start()
             each(rows_below, lambda m: coef_copy(1, m).start())
             own_tile(1)
 
@@ -560,7 +584,6 @@
                 image_copy(a, d, h).wait_send()
         for d in range(SLAB):
             farcross_copy(a, d).wait_send()
-        sibling_copy(a).wait_send()
         each(rows_below, lambda m: coef_copy(a, m).wait_send())
         each(rows_above, lambda m: farback_copy(a, m).wait_send())
 
@@ -578,8 +601,11 @@
 
     for d in range(1, SLAB):
         dense_copy(d).wait_send()
+        share_copy(d).wait_send()
+    sibling_copy().wait_send()
     for d in range(SLAB):
         dense_cross_copy(d).wait_send()
+        share_cross_copy(d).wait_send()
 
 
 def per_device(n_rows, *arrays):

time: 47.3 us -> 45.9 us (0.970)
  Pallas kernels: 43.7 us -> 42.4 us
    pallas_call x1, Pallas kernels: 43.7 us -> 42.4 us  [per_device(): pl.pallas_call(functools.partial(kernel, n_rows), out_shape=(image, image...]
where the time goes in v4:
time: 45.9 us; the launch traced here: 45.7 us
  Pallas kernels  42.4 us (92%)
  between operations  1.93 us (4%)
  local copies, waits for them, and re-layouts  1.41 us (3%)
    pallas_call x1, Pallas kernels, per_device(): pl.pallas_call(functools.partial(kernel, n_rows), out_shape=(image, image...  42.4 us
    unnamed x2, local copies, waits for them, and re-layouts  1.41 us

profile of v4, /device:TPU:1, one launch (start us, length us, event | category | flops | bytes accessed | tf_op | source)
XLA Modules:
  0.0 45.7 jit_solution(14236886391244199625)
XLA Ops:
  1.9 42.4 %shard_map.122 = (bf16[4,128,256]{2,1,0:T(8,128)(2,1)S(1)}, bf16[4,128,256]{2,1,0:T(8,128)(2,1)S(1)}) custom-call(bf16[4,128,256]{2,1,0:T(8,128)(2,1)} %charges_hbm.1, bf16[4,32,256]{2,1,0:T(8,128)(2,1)} %basis_hbm.1, s32[4]{0:T(128)} %sizes_hbm.1, bf16[16,256,256]{2,1,0:T(8,128)(2,1)} %blocks_hbm.1, s32[16]{0:T(128)} %near_rows_hbm.1, s32[16]{0:T(128)} %near_cols_hbm.1, ...), custom_call_target="tpu_custom_call" | custom-call | tf_op jit(solution)/shard_map/pallas_call | solution.py:620
  44.3 0.7 %copy.17 = bf16[4,128,256]{2,1,0:T(8,128)(2,1)} copy(bf16[4,128,256]{2,1,0:T(8,128)(2,1)S(1)} %get-tuple-element.4) | data formatting | bytes 524288
  45.0 0.7 %copy.18 = bf16[4,128,256]{2,1,0:T(8,128)(2,1)} copy(bf16[4,128,256]{2,1,0:T(8,128)(2,1)S(1)} %get-tuple-element.5) | data formatting | bytes 524288

commit v5 on v4

--- a/solution.py
+++ b/solution.py
@@ -477,6 +477,30 @@
         if at == PART_AT[a]:
             far_part(a)
 
+    def finish_early(a):
+        each(rows_below, lambda m: coef_copy(a, m).wait_send())
+        each(rows_above, lambda m: farback_copy(a, m).wait_send())
+
+        @pl.when(has_below)
+        def _():
+            for turn in range(SLAB):
+                for h in range(2):
+                    field_copy(a, turn, h).wait_send()
+
+        @pl.when(has_above)
+        def _():
+            for turn in range(SLAB):
+                for h in range(2):
+                    ahead_copy(a, turn, h).wait_send()
+
+    def finish_parts(a):
+        for d in range(1, SLAB):
+            farpart_copy(a, d).wait_send()
+            for h in range(2):
+                part_copy(a, d, h).wait_send()
+        for d in range(SLAB):
+            farcross_copy(a, d).wait_send()
+
     for a in range(2):
         for h in range(2):
             if a == 1:
@@ -528,6 +552,22 @@
 
         far_total = farpart_send[a, ranks(c), :].astype(F32)
         far_total = far_total + jnp.where(odd == 1, farback_send[a, 0:RANK, :], 0).astype(F32)
+
+        if a == 1:
+            for h in range(2):
+                first_image[:, halves[h], :] = own[1][h][...]
+                for d in range(1, SLAB):
+                    image_copy(0, d, h).wait_send()
+            for d in range(1, SLAB):
+                dense_copy(d).wait_send()
+                share_copy(d).wait_send()
+            for d in range(SLAB):
+                dense_cross_copy(d).wait_send()
+                share_cross_copy(d).wait_send()
+            sibling_copy().wait_send()
+            finish_early(0)
+            finish_parts(0)
+            finish_early(1)
 
         each(rows_below, lambda m: farback_copy(a, m).wait_recv())
         for m in range(TILES):
@@ -571,41 +611,14 @@
             each(rows_below, lambda m: coef_copy(1, m).start())
             own_tile(1)
 
+    finish_parts(1)
     for h in range(2):
-        first_image[:, halves[h], :] = own[1][h][...]
         for d in (1, 3, 2):
             image_copy(1, d, h).wait_recv()
 
-    for a in range(2):
+    for h in range(2):
         for d in range(1, SLAB):
-            farpart_copy(a, d).wait_send()
-            for h in range(2):
-                part_copy(a, d, h).wait_send()
-                image_copy(a, d, h).wait_send()
-        for d in range(SLAB):
-            farcross_copy(a, d).wait_send()
-        each(rows_below, lambda m: coef_copy(a, m).wait_send())
-        each(rows_above, lambda m: farback_copy(a, m).wait_send())
-
-        @pl.when(has_below)
-        def _():
-            for turn in range(SLAB):
-                for h in range(2):
-                    field_copy(a, turn, h).wait_send()
-
-        @pl.when(has_above)
-        def _():
-            for turn in range(SLAB):
-                for h in range(2):
-                    ahead_copy(a, turn, h).wait_send()
-
-    for d in range(1, SLAB):
-        dense_copy(d).wait_send()
-        share_copy(d).wait_send()
-    sibling_copy().wait_send()
-    for d in range(SLAB):
-        dense_cross_copy(d).wait_send()
-        share_cross_copy(d).wait_send()
+            image_copy(1, d, h).wait_send()
 
 
 def per_device(n_rows, *arrays):

time: 45.9 us -> 45.7 us (level)
  no operation moved by 1% of the time
where the time goes in v5:
time: 45.7 us; the launch traced here: 45.5 us
  Pallas kernels  42.2 us (92%)
  between operations  1.93 us (4%)
  local copies, waits for them, and re-layouts  1.41 us (3%)
    pallas_call x1, Pallas kernels, per_device(): pl.pallas_call(functools.partial(kernel, n_rows), out_shape=(image, image...  42.2 us
    unnamed x2, local copies, waits for them, and re-layouts  1.41 us

profile of v5, /device:TPU:1, one launch (start us, length us, event | category | flops | bytes accessed | tf_op | source)
XLA Modules:
  0.0 45.5 jit_solution(6344368595033781601)
XLA Ops:
  1.9 42.2 %shard_map.122 = (bf16[4,128,256]{2,1,0:T(8,128)(2,1)S(1)}, bf16[4,128,256]{2,1,0:T(8,128)(2,1)S(1)}) custom-call(bf16[4,128,256]{2,1,0:T(8,128)(2,1)} %charges_hbm.1, bf16[4,32,256]{2,1,0:T(8,128)(2,1)} %basis_hbm.1, s32[4]{0:T(128)} %sizes_hbm.1, bf16[16,256,256]{2,1,0:T(8,128)(2,1)} %blocks_hbm.1, s32[16]{0:T(128)} %near_rows_hbm.1, s32[16]{0:T(128)} %near_cols_hbm.1, ...), custom_call_target="tpu_custom_call" | custom-call | tf_op jit(solution)/shard_map/pallas_call | solution.py:633
  44.1 0.7 %copy.17 = bf16[4,128,256]{2,1,0:T(8,128)(2,1)} copy(bf16[4,128,256]{2,1,0:T(8,128)(2,1)S(1)} %get-tuple-element.4) | data formatting | bytes 524288
  44.8 0.7 %copy.18 = bf16[4,128,256]{2,1,0:T(8,128)(2,1)} copy(bf16[4,128,256]{2,1,0:T(8,128)(2,1)S(1)} %get-tuple-element.5) | data formatting | bytes 524288
